TPU v7x, 32 devices: a whole 2x2x4 slice. The times are simulated.
32 devices in a mesh: member: 8 (over y, x, core), region: 4 (over z).
Axes of the slice: x: 2, y: 2, z: 4, core: 2. Of those that a mesh axis runs over, the one named last changes fastest.
Arguments:
- ensemble: float32 [256, 76, 2048], P('member', None, 'region'), may hold values from -6 to 6
- blending_matrix: float32 [76, 76], replicated, may hold values from -0.625 to 0.625
- lateral_spreading: float32 [76], replicated, may hold values from 0.19 to 0.2
- obs_op: float32 [256, 128, 608], P(('region', 'member')), may hold values from -0.25 to 0.25
- obs_value: float32 [256, 128], P(('region', 'member')), may hold values from -6 to 6
- obs_precision: float32 [256, 128], P(('region', 'member')), may hold values from 0.01 to 3000
Outputs:
- analysis: float32 [256, 76, 2048], P('member', None, 'region')
All inputs are finite; a program needn't handle non-finite values.
Results may differ from a plain program's by a relative error of at most 0.0003.
Values sent between devices are 32-bit elements; how exact they have to be, the bound alone decides.
A program may use at most 192 MiB of HBM per device.

v0:
```python
import math

import jax
import jax.numpy as jnp
from jax import lax
from jax.sharding import PartitionSpec as P

GY = 128
NSTEP = 4
ITERS = 12


HIGHEST = lax.Precision.HIGHEST


def extended(cells, sides, width):
    for axis, dim in sides:
        count = lax.axis_size(axis)
        head = lax.slice_in_dim(cells, 0, width, axis=dim)
        tail = lax.slice_in_dim(cells, cells.shape[dim] - width, cells.shape[dim], axis=dim)
        cells = jnp.concatenate(
            [
                lax.ppermute(tail, axis, [(i, (i + 1) % count) for i in range(count)]),
                cells,
                lax.ppermute(head, axis, [((i + 1) % count, i) for i in range(count)]),
            ],
            axis=dim,
        )
    return cells


def analyse(packed):
    patch_state, operator, observed, precisions = packed
    ens_size = patch_state.shape[0]
    mean_state = jnp.mean(patch_state, axis=0)
    perturb = patch_state - mean_state
    obs_pert = jnp.dot(perturb, operator.T, precision=HIGHEST, preferred_element_type=jnp.float32)
    obs_mean = jnp.dot(operator, mean_state, precision=HIGHEST, preferred_element_type=jnp.float32)
    innovation = observed - obs_mean
    weighted = obs_pert * precisions
    gram_matrix = jnp.dot(
        weighted, obs_pert.T, precision=HIGHEST, preferred_element_type=jnp.float32
    )
    identity = jnp.eye(ens_size, dtype=jnp.float32)
    system = (ens_size - 1.0) * identity + gram_matrix
    norm_scale = jnp.sqrt(jnp.sum(system * system))
    sqrt_iter = system / norm_scale
    inv_iter = identity
    for step_index in range(ITERS):
        factor = 0.5 * (
            3.0 * identity
            - jnp.dot(inv_iter, sqrt_iter, precision=HIGHEST, preferred_element_type=jnp.float32)
        )
        sqrt_iter = jnp.dot(
            sqrt_iter, factor, precision=HIGHEST, preferred_element_type=jnp.float32
        )
        inv_iter = jnp.dot(factor, inv_iter, precision=HIGHEST, preferred_element_type=jnp.float32)
    inv_sqrt = inv_iter / jnp.sqrt(norm_scale)
    inverse = jnp.dot(inv_sqrt, inv_sqrt, precision=HIGHEST, preferred_element_type=jnp.float32)
    mean_w = jnp.dot(
        inverse,
        jnp.dot(weighted, innovation, precision=HIGHEST, preferred_element_type=jnp.float32),
        precision=HIGHEST,
        preferred_element_type=jnp.float32,
    )
    weights = math.sqrt(ens_size - 1.0) * inv_sqrt + mean_w[:, None]
    return mean_state + jnp.dot(
        weights.T, perturb, precision=HIGHEST, preferred_element_type=jnp.float32
    )


def shards(ensemble, blending_matrix, lateral_spreading, obs_op, obs_value, obs_precision):
    mem_dev, levels, cols_dev = ensemble.shape
    row_count = cols_dev // GY
    layered_variables = ensemble.reshape(mem_dev, levels, row_count, GY)
    diffuse_rate = lateral_spreading[None, :, None, None]
    for step_index in range(NSTEP):
        padded = extended(layered_variables, (("region", 2),), 1)
        centre = padded[:, :, 1:-1, :]
        laplace = (
            padded[:, :, 2:, :]
            + padded[:, :, :-2, :]
            + jnp.roll(centre, -1, 3)
            + jnp.roll(centre, 1, 3)
            - 4.0 * centre
        )
        coupled = jnp.einsum("fg,mgxy->mfxy", blending_matrix, centre, precision=HIGHEST)
        layered_variables = centre + diffuse_rate * laplace + 0.3 * jnp.tanh(coupled)
    members = lax.axis_size("member")
    patch_count = obs_op.shape[0]
    patch_cols = cols_dev // (members * patch_count)
    entry_width = mem_dev * levels * patch_cols
    split_cols = layered_variables.reshape(mem_dev, levels, members, patch_count, patch_cols)
    outgoing = split_cols.transpose(2, 3, 0, 1, 4).reshape(members, patch_count, entry_width)
    at_owner = lax.all_to_all(outgoing, "member", split_axis=0, concat_axis=2, tiled=True)
    ens_total = mem_dev * members
    neighbourhood_tiles = at_owner.reshape(patch_count, ens_total, levels * patch_cols)
    result = lax.map(analyse, (neighbourhood_tiles, obs_op, obs_value, obs_precision))
    backward = result.reshape(patch_count, members, entry_width)
    returned = lax.all_to_all(backward, "member", split_axis=1, concat_axis=0, tiled=True)
    restored = returned.reshape(members, patch_count, mem_dev, levels, patch_cols).transpose(
        2, 3, 0, 1, 4
    )
    return restored.reshape(mem_dev, levels, cols_dev)


def solution(mesh):
    return jax.shard_map(
        shards,
        mesh=mesh,
        in_specs=(
            P("member", None, "region"),
            P(),
            P(),
            P(("region", "member"), None, None),
            P(("region", "member"), None),
            P(("region", "member"), None),
        ),
        out_specs=P("member", None, "region"),
        check_vma=False,
    )
```

profile of v0, /device:TPU:0, one launch (start us, length us, event | category | flops | bytes accessed | tf_op | source)
XLA Modules:
  0.0 953.5 jit_solution(18124865899235556619)
XLA Ops:
  0.0 6.8 reshape.35
  33.4 13.0 %collective-permute-done = f32[32,76,1,128]{3,0,2,1:T(8,128)S(1)} collective-permute-done((f32[32,76,1,128]{3,0,2,1:T(8,128)S(1)}, f32[32,76,1,128]{3,0,2,1:T(8,128)S(1)}, u32[]{:S(2)}, u32[]{:S(2)}) %collective-permute-start) | collective-permute-done | bytes 1245216 | tf_op jit(solution)/shard_map/ppermute | solution.py:25
  47.2 25.7 %collective-permute-done.1 = f32[32,76,1,128]{3,0,2,1:T(8,128)S(1)} collective-permute-done((f32[32,76,1,128]{3,0,2,1:T(8,128)S(1)}, f32[32,76,1,128]{3,0,2,1:T(8,128)S(1)}, u32[]{:S(2)}, u32[]{:S(2)}) %collective-permute-start.1) | collective-permute-done | bytes 1245216 | tf_op jit(solution)/shard_map/ppermute | solution.py:23
  73.6 22.3 %fusion.70 = f32[32,76,4,128]{3,1,2,0:T(8,128)} fusion(f32[32,76,4,128]{3,1,2,0:T(8,128)} %copy-done.5, f32[32,76,1,128]{3,1,2,0:T(8,128)S(1)} %copy.30, f32[32,76,1,128]{3,1,2,0:T(8,128)S(1)} %copy.28, f32[32,76,4,1]{3,1,2,0:T(8,128)} %get-tuple-element.83, f32[32,76,4,127]{3,1,2,0:T(8,128)} %get-tuple-element.85, ...), kind=kOutput, calls=%fused_computation.102 | convolution fusion | flops 1151795200 | bytes 22436720 | tf_op jit(solution)/shard_map/fg,mgxy->mfxy/dot_general | solution.py:87
  112.8 16.7 %collective-permute-done.2 = f32[32,76,1,128]{3,0,2,1:T(8,128)S(1)} collective-permute-done((f32[32,76,1,128]{3,0,2,1:T(8,128)S(1)}, f32[32,76,1,128]{3,0,2,1:T(8,128)S(1)}, u32[]{:S(2)}, u32[]{:S(2)}) %collective-permute-start.2) | collective-permute-done | bytes 1245216 | tf_op jit(solution)/shard_map/ppermute | solution.py:25
  130.2 23.2 %collective-permute-done.3 = f32[32,76,1,128]{3,0,2,1:T(8,128)S(1)} collective-permute-done((f32[32,76,1,128]{3,0,2,1:T(8,128)S(1)}, f32[32,76,1,128]{3,0,2,1:T(8,128)S(1)}, u32[]{:S(2)}, u32[]{:S(2)}) %collective-permute-start.3) | collective-permute-done | bytes 1245216 | tf_op jit(solution)/shard_map/ppermute | solution.py:23
  154.1 22.4 %fusion.63 = f32[32,76,4,128]{3,1,2,0:T(8,128)} fusion(f32[32,76,4,128]{3,1,2,0:T(8,128)} %fusion.70, f32[32,76,1,128]{3,1,2,0:T(8,128)S(1)} %copy.42, f32[32,76,1,128]{3,1,2,0:T(8,128)S(1)} %copy.40, f32[32,76,4,1]{3,1,2,0:T(8,128)} %get-tuple-element.77, f32[32,76,4,127]{3,1,2,0:T(8,128)} %get-tuple-element.79, f32[32,76,4,127]{3,1,2,0:T(8,128)} %get-tuple-element.78, ...), kind=kOutput, calls=%fused_computation.93 | convolution fusion | flops 1151795200 | bytes 22436720 | tf_op jit(solution)/shard_map/fg,mgxy->mfxy/dot_general | solution.py:87
  194.4 15.5 %collective-permute-done.4 = f32[32,76,1,128]{3,0,2,1:T(8,128)S(1)} collective-permute-done((f32[32,76,1,128]{3,0,2,1:T(8,128)S(1)}, f32[32,76,1,128]{3,0,2,1:T(8,128)S(1)}, u32[]{:S(2)}, u32[]{:S(2)}) %collective-permute-start.4) | collective-permute-done | bytes 1245216 | tf_op jit(solution)/shard_map/ppermute | solution.py:25
  210.6 26.2 %collective-permute-done.5 = f32[32,76,1,128]{3,0,2,1:T(8,128)S(1)} collective-permute-done((f32[32,76,1,128]{3,0,2,1:T(8,128)S(1)}, f32[32,76,1,128]{3,0,2,1:T(8,128)S(1)}, u32[]{:S(2)}, u32[]{:S(2)}) %collective-permute-start.5) | collective-permute-done | bytes 1245216 | tf_op jit(solution)/shard_map/ppermute | solution.py:23
  237.5 22.3 %fusion.56 = f32[32,76,4,128]{3,1,2,0:T(8,128)} fusion(f32[32,76,4,128]{3,1,2,0:T(8,128)} %fusion.63, f32[32,76,1,128]{3,1,2,0:T(8,128)S(1)} %copy.46, f32[32,76,1,128]{3,1,2,0:T(8,128)S(1)} %copy.44, f32[32,76,4,1]{3,1,2,0:T(8,128)} %get-tuple-element.71, f32[32,76,4,127]{3,1,2,0:T(8,128)} %get-tuple-element.73, f32[32,76,4,127]{3,1,2,0:T(8,128)} %get-tuple-element.72, ...), kind=kOutput, calls=%fused_computation.84 | convolution fusion | flops 1151795200 | bytes 22436720 | tf_op jit(solution)/shard_map/fg,mgxy->mfxy/dot_general | solution.py:87
  276.8 15.5 %collective-permute-done.6 = f32[32,76,1,128]{3,0,2,1:T(8,128)S(1)} collective-permute-done((f32[32,76,1,128]{3,0,2,1:T(8,128)S(1)}, f32[32,76,1,128]{3,0,2,1:T(8,128)S(1)}, u32[]{:S(2)}, u32[]{:S(2)}) %collective-permute-start.6) | collective-permute-done | bytes 1245216 | tf_op jit(solution)/shard_map/ppermute | solution.py:25
  293.0 25.1 %collective-permute-done.7 = f32[32,76,1,128]{3,0,2,1:T(8,128)S(1)} collective-permute-done((f32[32,76,1,128]{3,0,2,1:T(8,128)S(1)}, f32[32,76,1,128]{3,0,2,1:T(8,128)S(1)}, u32[]{:S(2)}, u32[]{:S(2)}) %collective-permute-start.7) | collective-permute-done | bytes 1245216 | tf_op jit(solution)/shard_map/ppermute | solution.py:23
  318.8 22.4 %fusion.49 = f32[32,76,4,128]{3,1,2,0:T(8,128)} fusion(f32[32,76,4,128]{3,1,2,0:T(8,128)} %fusion.56, f32[32,76,1,128]{3,1,2,0:T(8,128)S(1)} %copy.50, f32[32,76,1,128]{3,1,2,0:T(8,128)S(1)} %copy.48, f32[32,76,4,1]{3,1,2,0:T(8,128)} %get-tuple-element.65, f32[32,76,4,127]{3,1,2,0:T(8,128)} %get-tuple-element.67, f32[32,76,4,127]{3,1,2,0:T(8,128)} %get-tuple-element.66, ...), kind=kOutput, calls=%fused_computation.75 | convolution fusion | flops 1151795200 | bytes 22436720 | tf_op jit(solution)/shard_map/fg,mgxy->mfxy/dot_general | solution.py:87
  341.2 7.8 copy.51
  349.0 40.2 %copy.52 = f32[8,8,32,76,8]{4,3,2,1,0:T(8,128)} copy(f32[8,8,32,76,8]{3,4,1,0,2:T(8,128)} %bitcast.319) | data formatting | bytes 9961472 | tf_op jit(solution)/shard_map/transpose | solution.py:94
  389.2 69.1 %reshape.37 = f32[8,8,19456]{2,1,0:T(8,128)} reshape(f32[8,8,32,76,8]{4,3,2,1,0:T(8,128)} %copy.52) | data formatting | bytes 9961472 | tf_op jit(solution)/shard_map/reshape | solution.py:94
  463.0 57.5 %all-to-all-done = f32[8,8,19456]{2,1,0:T(8,128)} async-done(((f32[8,8,19456]{2,1,0:T(8,128)}), f32[8,8,19456]{2,1,0:T(8,128)}, u32[]{:S(2)}, u32[]{:S(2)}) %all-to-all-start) | async-done | bytes 4980768 | tf_op jit(solution)/shard_map/all_to_all | solution.py:95
  520.5 7.5 copy.53
  528.1 6.8 reshape.38
  540.7 195.6 %while.10 = (s32[]{:T(128)}, f32[8,256,608]{1,2,0:T(8,128)}, f32[8,256,608]{1,2,0:T(8,128)}, f32[8,128,608]{1,2,0:T(8,128)}, f32[8,128]{1,0:T(8,128)}, /*index=5*/f32[8,128]{1,0:T(8,128)}, s32[]{:T(128)}) while((s32[]{:T(128)}, f32[8,256,608]{1,2,0:T(8,128)}, f32[8,256,608]{1,2,0:T(8,128)}, f32[8,128,608]{1,2,0:T(8,128)}, f32[8,128]{1,0:T(8,128)}, ...), condition=%wide.region_3.4_spmd, body=%wide.region_0.3_spmd.sunk | while | flops 8072380416 | bytes 31853812 | solution.py:98
  754.1 60.8 %all_to_all.30 = f32[8,8,19456]{2,0,1:T(8,128)} all-to-all(f32[8,8,19456]{2,0,1:T(8,128)S(1)} %copy.56), channel_id=1, replica_groups=mesh['member'=8,'region'=4] {'member'}, dimensions={1} | all-to-all | bytes 9961472 | tf_op jit(solution)/shard_map/all_to_all | solution.py:100
  814.9 83.5 %reshape.40 = f32[8,8,32,76,8]{4,3,2,1,0:T(8,128)} reshape(f32[8,8,1,19456]{3,1,0,2:T(8,128)} %bitcast.320) | data formatting | bytes 9961472 | tf_op jit(solution)/shard_map/reshape | solution.py:101
  898.4 45.6 %copy.57 = f32[32,76,8,8,8]{1,4,3,2,0:T(8,128)} copy(f32[32,76,8,8,8]{4,1,0,3,2:T(8,128)} %bitcast.26) | data formatting | bytes 9961472 | tf_op jit(solution)/shard_map/transpose | solution.py:101
  944.0 9.1 copy.58
  (425 shorter events, 299.8 us)
Async XLA Ops:
  0.0 73.6 %copy-start = (f32[76,76]{1,0:T(8,128)S(1)}, f32[76,76]{1,0:T(8,128)}, u32[]{:S(2)}) copy-start(f32[76,76]{1,0:T(8,128)} %param.9) | copy-start | bytes 69316
  6.8 11.9 %copy-start.6 = (f32[32,76,4,128]{3,2,0,1:T(4,128)S(1)}, f32[32,76,4,128]{3,2,0,1:T(4,128)}, u32[]{:S(2)}) copy-start(f32[32,76,4,128]{3,2,0,1:T(4,128)} %reshape.35) | copy-start | bytes 14942212
  13.6 32.9 %collective-permute-start = (f32[32,76,1,128]{3,0,2,1:T(8,128)S(1)}, f32[32,76,1,128]{3,0,2,1:T(8,128)S(1)}, u32[]{:S(2)}, u32[]{:S(2)}) collective-permute-start(f32[32,76,1,128]{3,0,2,1:T(8,128)S(1)} %bitcast.322), channel_id=1, source_target_pairs={{1,0},{2,1},{3,2},{0,3},{5,4},{6,5},{7,6},{4,7},{9,8},{10,9},{11,1... | collective-permute-start | bytes 3735560 | tf_op jit(solution)/shard_map/ppermute | solution.py:25
  18.7 54.2 %collective-permute-start.1 = (f32[32,76,1,128]{3,0,2,1:T(8,128)S(1)}, f32[32,76,1,128]{3,0,2,1:T(8,128)S(1)}, u32[]{:S(2)}, u32[]{:S(2)}) collective-permute-start(f32[32,76,1,128]{3,0,2,1:T(8,128)S(1)} %bitcast.321), channel_id=1, source_target_pairs={{0,1},{1,2},{2,3},{3,0},{4,5},{5,6},{6,7},{7,4},{8,9},{9,10},{10,1... | collective-permute-start | bytes 3735560 | tf_op jit(solution)/shard_map/ppermute | solution.py:23
  21.6 5.9 copy-start.5
  27.5 46.2 %copy-start.7 = (f32[76]{0:T(128)S(1)}, f32[76]{0:T(128)}, u32[]{:S(2)}) copy-start(f32[76]{0:T(128)} %param.10) | copy-start | bytes 916
  96.0 5.0 copy-start.2
  98.4 31.0 %collective-permute-start.2 = (f32[32,76,1,128]{3,0,2,1:T(8,128)S(1)}, f32[32,76,1,128]{3,0,2,1:T(8,128)S(1)}, u32[]{:S(2)}, u32[]{:S(2)}) collective-permute-start(f32[32,76,1,128]{3,0,2,1:T(8,128)S(1)} %copy.39), channel_id=1, source_target_pairs={{1,0},{2,1},{3,2},{0,3},{5,4},{6,5},{7,6},{4,7},{9,8},{10,9},{11,1... | collective-permute-start | bytes 3735560 | tf_op jit(solution)/shard_map/ppermute | solution.py:25
  100.6 52.8 %collective-permute-start.3 = (f32[32,76,1,128]{3,0,2,1:T(8,128)S(1)}, f32[32,76,1,128]{3,0,2,1:T(8,128)S(1)}, u32[]{:S(2)}, u32[]{:S(2)}) collective-permute-start(f32[32,76,1,128]{3,0,2,1:T(8,128)S(1)} %copy.41), channel_id=1, source_target_pairs={{0,1},{1,2},{2,3},{3,0},{4,5},{5,6},{6,7},{7,4},{8,9},{9,10},{10,1... | collective-permute-start | bytes 3735560 | tf_op jit(solution)/shard_map/ppermute | solution.py:23
  176.5 6.0 copy-start.3
  179.0 30.9 %collective-permute-start.4 = (f32[32,76,1,128]{3,0,2,1:T(8,128)S(1)}, f32[32,76,1,128]{3,0,2,1:T(8,128)S(1)}, u32[]{:S(2)}, u32[]{:S(2)}) collective-permute-start(f32[32,76,1,128]{3,0,2,1:T(8,128)S(1)} %copy.43), channel_id=1, source_target_pairs={{1,0},{2,1},{3,2},{0,3},{5,4},{6,5},{7,6},{4,7},{9,8},{10,9},{11,1... | collective-permute-start | bytes 3735560 | tf_op jit(solution)/shard_map/ppermute | solution.py:25
  182.5 54.3 %collective-permute-start.5 = (f32[32,76,1,128]{3,0,2,1:T(8,128)S(1)}, f32[32,76,1,128]{3,0,2,1:T(8,128)S(1)}, u32[]{:S(2)}, u32[]{:S(2)}) collective-permute-start(f32[32,76,1,128]{3,0,2,1:T(8,128)S(1)} %copy.45), channel_id=1, source_target_pairs={{0,1},{1,2},{2,3},{3,0},{4,5},{5,6},{6,7},{7,4},{8,9},{9,10},{10,1... | collective-permute-start | bytes 3735560 | tf_op jit(solution)/shard_map/ppermute | solution.py:23
  259.8 5.2 copy-start.4
  262.2 30.1 %collective-permute-start.6 = (f32[32,76,1,128]{3,0,2,1:T(8,128)S(1)}, f32[32,76,1,128]{3,0,2,1:T(8,128)S(1)}, u32[]{:S(2)}, u32[]{:S(2)}) collective-permute-start(f32[32,76,1,128]{3,0,2,1:T(8,128)S(1)} %copy.47), channel_id=1, source_target_pairs={{1,0},{2,1},{3,2},{0,3},{5,4},{6,5},{7,6},{4,7},{9,8},{10,9},{11,1... | collective-permute-start | bytes 3735560 | tf_op jit(solution)/shard_map/ppermute | solution.py:25
  264.9 53.2 %collective-permute-start.7 = (f32[32,76,1,128]{3,0,2,1:T(8,128)S(1)}, f32[32,76,1,128]{3,0,2,1:T(8,128)S(1)}, u32[]{:S(2)}, u32[]{:S(2)}) collective-permute-start(f32[32,76,1,128]{3,0,2,1:T(8,128)S(1)} %copy.49), channel_id=1, source_target_pairs={{0,1},{1,2},{2,3},{3,0},{4,5},{5,6},{6,7},{7,4},{8,9},{9,10},{10,1... | collective-permute-start | bytes 3735560 | tf_op jit(solution)/shard_map/ppermute | solution.py:23
  458.3 62.2 %all-to-all-start = ((f32[8,8,19456]{2,1,0:T(8,128)}), f32[8,8,19456]{2,1,0:T(8,128)}, u32[]{:S(2)}, u32[]{:S(2)}) async-start(f32[8,8,19456]{2,1,0:T(8,128)} %reshape.37), calls=%async_computation | async-start | bytes 9961472 | tf_op jit(solution)/shard_map/all_to_all | solution.py:95
  944.0 9.1 copy-start.1
where the time goes:
time: 966 us; the launch traced here: 953 us
  local copies, waits for them, and re-layouts  377 us (39%)
  matrix products  261 us (27%)
  waiting for transfers between devices  218 us (23%)
  blocking collectives  60.8 us (6%)
  starting transfers between devices  17.3 us (2%)
  other arithmetic  10 us (1%)
    ppermute x4, waiting for transfers between devices, extended(): lax.ppermute(tail, axis, [(i, (i + 1) % count) for i in range(count)])  100 us
    dot_general x4, matrix products, shards(): jnp.einsum('fg,mgxy->mfxy', blending_matrix, centre, precision=HIGHEST)  89.3 us
    reshape x1, local copies, waits for them, and re-layouts, shards(): returned.reshape(members, patch_count, mem_dev, levels, patch_cols)  83.5 us
    reshape x1, local copies, waits for them, and re-layouts, shards(): split_cols.transpose(2, 3, 0, 1, 4)  69.1 us
    all_to_all x1, blocking collectives, shards(): lax.all_to_all(backward, 'member', split_axis=1, concat_axis=0, tiled=True)  60.8 us
    ppermute x4, waiting for transfers between devices, extended(): lax.ppermute(head, axis, [((i + 1) % count, i) for i in range(count)])  60.7 us
    all_to_all x1, waiting for transfers between devices, shards(): lax.all_to_all(outgoing, 'member', split_axis=0, concat_axis=2, tiled=True)  57.5 us
    slice x8, local copies, waits for them, and re-layouts, shards(): jnp.roll(centre, 1, 3)  47.3 us
  transfers between devices with their start and end apart: 9, of which 9 were waited for; matrix products, arithmetic and copies ran while one was open for 6% of the time, Pallas kernels for 0%

commit v1 on v0

v1 whole, which is shorter than its diff:
```python
import functools
import math

import jax
import jax.numpy as jnp
from jax import lax
from jax.experimental import pallas as pl
from jax.experimental.pallas import tpu as pltpu
from jax.sharding import PartitionSpec as P

GY = 128
NSTEP = 4
ITERS = 12
HIGHEST = lax.Precision.HIGHEST
F32 = jnp.float32
BF16 = jnp.bfloat16
VMEM = pl.BlockSpec(memory_space=pltpu.VMEM)
PARAMS = pltpu.CompilerParams(vmem_limit_bytes=56 * 2**20)


def mm(a, b):
    return jnp.dot(a, b, preferred_element_type=F32)


def split2(x):
    hi = x.astype(BF16)
    return hi, (x - hi.astype(F32)).astype(BF16)


def split3(x):
    hi = x.astype(BF16)
    rest = x - hi.astype(F32)
    mid = rest.astype(BF16)
    return hi, mid, (rest - mid.astype(F32)).astype(BF16)


def dot3(a, b):
    a0, a1 = split2(a)
    b0, b1 = split2(b)
    return mm(a0, b0) + (mm(a0, b1) + mm(a1, b0))


def dot6(a, b):
    a0, a1, a2 = split3(a)
    b0, b1, b2 = split3(b)
    left = jnp.concatenate([a0, a1], 1)
    low = mm(jnp.concatenate([a0, a2], 1), jnp.concatenate([b2, b0], 0))
    low = low + mm(left, jnp.concatenate([b1, b0], 0))
    return low + mm(left, jnp.concatenate([b0, b1], 0))


def mixing(blend_ref, levels):
    padded = blend_ref.shape[0]
    hi, lo = split2(blend_ref[...])
    lane = lax.broadcasted_iota(jnp.int32, blend_ref.shape, 1)
    return jnp.where(lane < 2 * padded, hi.astype(F32), lo.astype(F32)).astype(BF16)


def advance(x, up, down, mix, rate):
    levels = x.shape[0]
    padded = mix.shape[0]
    full = jnp.concatenate([x, jnp.zeros((padded - levels, x.shape[1]), F32)], 0)
    hi, lo = split2(full)
    coupled = mm(mix, jnp.concatenate([hi, lo, hi], 0))[:levels]
    rows = x.shape[1] // GY
    parts = [x[:, r * GY:(r + 1) * GY] for r in range(rows)]
    ext = [up] + parts + [down]
    out = []
    for r in range(rows):
        c = parts[r]
        lap = ext[r] + ext[r + 2] + pltpu.roll(c, 1, 1) + pltpu.roll(c, GY - 1, 1) - 4.0 * c
        out.append(c + rate * lap + 0.3 * jnp.tanh(coupled[:, r * GY:(r + 1) * GY]))
    return out


def step_kernel(x_ref, up_ref, down_ref, blend_ref, rate_ref, o_ref, head_ref, tail_ref):
    levels = x_ref.shape[1]
    mix = mixing(blend_ref, levels)
    rate = rate_ref[...]

    @pl.loop(0, x_ref.shape[0])
    def _(m):
        new = advance(x_ref[m], up_ref[m], down_ref[m], mix, rate)
        for r, part in enumerate(new):
            o_ref[m, :, r * GY:(r + 1) * GY] = part
        head_ref[m] = new[0]
        tail_ref[m] = new[-1]


def rows_of(i, levels, stride):
    return pl.ds(i, levels) if stride == 1 else pl.ds(i, levels, stride=stride)


def last_kernel(x_ref, up_ref, down_ref, blend_ref, rate_ref, o_ref):
    mem, levels, cols = x_ref.shape
    rows = cols // GY
    pack = o_ref.shape[0] // rows
    width = GY // pack
    group = mem // pack
    mix = mixing(blend_ref, levels)
    rate = rate_ref[...]
    place = lax.broadcasted_iota(jnp.int32, (levels, GY), 1) // width

    def body(i):
        news = []
        for h in range(pack):
            m = h * group + i
            news.append(advance(x_ref[m], up_ref[m], down_ref[m], mix, rate))
        for r in range(rows):
            for c in range(pack):
                value = news[c][r]
                for h in range(pack):
                    if h != c:
                        moved = pltpu.roll(news[h][r], (h - c) * width % GY, 1)
                        value = jnp.where(place == h, moved, value)
                o_ref[r * pack + c, rows_of(i, levels, group), :] = value

    if group == 1:
        body(0)
    else:
        pl.loop(0, group)(body)


def unpack_kernel(x_ref, o_ref):
    mem, levels, cols = o_ref.shape
    rows = cols // GY
    pack = x_ref.shape[0] // rows
    width = GY // pack
    group = mem // pack
    place = lax.broadcasted_iota(jnp.int32, (levels, GY), 1) // width

    def body(i):
        for r in range(rows):
            got = [x_ref[r * pack + c, rows_of(i, levels, group), :] for c in range(pack)]
            for h in range(pack):
                value = got[h]
                for c in range(pack):
                    if c != h:
                        value = jnp.where(place == c, pltpu.roll(got[c], (c - h) * width % GY, 1), value)
                o_ref[h * group + i, :, r * GY:(r + 1) * GY] = value

    if group == 1:
        body(0)
    else:
        pl.loop(0, group)(body)


def analysis_kernel(levels, x_ref, op_ref, val_ref, prec_ref, o_ref,
                    xt_ref, mean_ref, u_ref, v_ref, state_ref, scal_ref):
    sources, packed, _ = x_ref.shape
    group = packed // levels
    patches, nobs, entries = op_ref.shape
    cells = entries // levels
    ens = xt_ref.shape[2]
    width = patches * cells
    pack = GY // width
    half = sources * group
    a = ens - 1.0
    eye = (lax.broadcasted_iota(jnp.int32, (nobs, nobs), 0)
           == lax.broadcasted_iota(jnp.int32, (nobs, nobs), 1)).astype(F32)

    @pl.loop(0, levels)
    def _(f):
        if group == 1:
            x = x_ref[:, f, :]
        else:
            x = x_ref[:, pl.ds(pl.multiple_of(f * group, group), group), :].reshape(half, GY)
        t = x.T
        for h in range(pack):
            for p in range(patches):
                xt_ref[p, pl.ds(pl.multiple_of(f * cells, cells), cells), h * half:(h + 1) * half] = (
                    t[h * width + p * cells:h * width + (p + 1) * cells, :])

    @pl.loop(0, patches)
    def _(p):
        x = xt_ref[p]
        mean = jnp.sum(x, axis=1, keepdims=True) * (1.0 / ens)
        e = x - mean
        xt_ref[p] = e
        mean_ref[p] = mean
        op = op_ref[p]
        obs_mean = jnp.dot(op, jnp.broadcast_to(mean, (entries, GY)), precision=HIGHEST,
                           preferred_element_type=F32)[:, :1]
        root = jnp.sqrt(prec_ref[p])
        u = dot3(op, e) * root
        u_ref[p] = u
        v_ref[p] = root * (val_ref[p] - obs_mean)
        gram = lax.dot_general(u, u, (((1,), (1,)), ((), ())), precision=HIGHEST,
                               preferred_element_type=F32)
        trace = jnp.sum(u * u, keepdims=True).reshape(1, 1)
        square = jnp.sum(gram * gram, keepdims=True).reshape(1, 1)
        s = jnp.sqrt(a * a * ens + 2.0 * a * trace + square)
        alpha = a / s
        state_ref[p, :, 0:nobs] = alpha * eye + gram / s
        state_ref[p, :, nobs:2 * nobs] = eye
        state_ref[p, :, 2 * nobs:3 * nobs] = jnp.zeros_like(eye)
        scal_ref[p, 0:1, :] = jnp.broadcast_to(s, (1, GY))
        scal_ref[p, 1:2, :] = jnp.broadcast_to(alpha, (1, GY))
        scal_ref[p, 2:3, :] = jnp.ones((1, GY), F32)

    @pl.loop(0, ITERS)
    def _(k):
        firsts = []
        for p in range(patches):
            state = state_ref[p]
            firsts.append(dot6(state[:, nobs:2 * nobs], state))
        for p in range(patches):
            first = firsts[p]
            alpha = scal_ref[p, 1:2, 0:1]
            z = scal_ref[p, 2:3, 0:1]
            factor = 1.5 * eye - 0.5 * first[:, 0:nobs]
            second = dot6(factor, state_ref[p])
            state_ref[p, :, 0:2 * nobs] = second[:, 0:2 * nobs]
            q = state_ref[p, :, 2 * nobs:3 * nobs]
            state_ref[p, :, 2 * nobs:3 * nobs] = second[:, 2 * nobs:3 * nobs] - 0.5 * z * (
                first[:, nobs:2 * nobs] + alpha * (first[:, 2 * nobs:3 * nobs] + z * q))
            scal_ref[p, 2:3, :] = jnp.broadcast_to(z * (1.5 - 0.5 * alpha * z * z), (1, GY))

    @pl.loop(0, patches)
    def _(p):
        s = scal_ref[p, 0:1, 0:1]
        z = scal_ref[p, 2:3, 0:1]
        scale = lax.rsqrt(s)
        root = state_ref[p, :, nobs:2 * nobs] * scale
        u = u_ref[p]
        once = jnp.sum(root * v_ref[p], axis=0, keepdims=True)
        twice = jnp.sum(root * once, axis=1, keepdims=True)
        w = jnp.sum(u * twice, axis=0, keepdims=True)
        e = xt_ref[p]
        qu = dot3(state_ref[p, :, 2 * nobs:3 * nobs], u) * (math.sqrt(a) * scale / s)
        weights = dot3(u.T, qu)
        shift = mean_ref[p] + jnp.sum(e * w, axis=1, keepdims=True)
        xt_ref[p] = shift + (math.sqrt(a) * scale * z) * e + dot3(e, weights)

    @pl.loop(0, levels)
    def _(f):
        t = jnp.concatenate([
            xt_ref[p, pl.ds(pl.multiple_of(f * cells, cells), cells), h * half:(h + 1) * half]
            for h in range(pack) for p in range(patches)], 0).T
        if group == 1:
            o_ref[:, f, :] = t
        else:
            o_ref[:, pl.ds(pl.multiple_of(f * group, group), group), :] = t.reshape(
                sources, group, GY)


def call(kernel, outs, args, scratch=(), params=PARAMS):
    return pl.pallas_call(
        kernel,
        out_shape=[jax.ShapeDtypeStruct(s, F32) for s in outs],
        in_specs=[VMEM] * len(args),
        out_specs=[VMEM] * len(outs),
        scratch_shapes=list(scratch),
        compiler_params=params,
    )(*args)


def shards(ensemble, blending_matrix, lateral_spreading, obs_op, obs_value, obs_precision):
    mem, levels, cols = ensemble.shape
    members = lax.axis_size("member")
    regions = lax.axis_size("region")
    patches, nobs, entries = obs_op.shape
    ens = mem * members
    pack = GY * members // cols
    padded = -(-levels // 16) * 16
    blend = jnp.tile(jnp.pad(blending_matrix, ((0, padded - levels),) * 2), (1, 3))
    rate = lateral_spreading[:, None]
    x, head, tail = ensemble, ensemble[:, :, :GY], ensemble[:, :, -GY:]
    for step in range(NSTEP):
        up = lax.ppermute(tail, "region", [(i, (i + 1) % regions) for i in range(regions)])
        down = lax.ppermute(head, "region", [((i + 1) % regions, i) for i in range(regions)])
        args = (x, up, down, blend, rate)
        if step < NSTEP - 1:
            side = (mem, levels, GY)
            x, head, tail = call(step_kernel, [x.shape, side, side], args)
    packed = (members, levels * mem // pack, GY)
    out, = call(last_kernel, [packed], args)
    got = lax.all_to_all(out, "member", split_axis=0, concat_axis=0, tiled=True)
    back, = call(
        functools.partial(analysis_kernel, levels), [packed],
        (got, obs_op, obs_value[:, :, None], obs_precision[:, :, None]),
        [
            pltpu.VMEM((patches, entries, ens), F32),
            pltpu.VMEM((patches, entries, 1), F32),
            pltpu.VMEM((patches, nobs, ens), F32),
            pltpu.VMEM((patches, nobs, 1), F32),
            pltpu.VMEM((patches, nobs, 3 * nobs), F32),
            pltpu.VMEM((patches, 8, GY), F32),
        ])
    back = lax.all_to_all(back, "member", split_axis=0, concat_axis=0, tiled=True)
    return call(unpack_kernel, [ensemble.shape], (back,))[0]


def solution(mesh):
    return jax.shard_map(
        shards,
        mesh=mesh,
        in_specs=(
            P("member", None, "region"),
            P(),
            P(),
            P(("region", "member"), None, None),
            P(("region", "member"), None),
            P(("region", "member"), None),
        ),
        out_specs=P("member", None, "region"),
        check_vma=False,
    )
```

time: 966 us -> 498 us (0.52); the launches traced: 953 us -> 497 us
  local copies, waits for them, and re-layouts: 377 us -> 44.1 us
  matrix products: 261 us -> 0 us
  Pallas kernels: 0 us -> 121 us
  waiting for transfers between devices: 218 us -> 246 us
  other arithmetic: 10 us -> 0 us
    dot_general x340 -> x0, matrix products: 261 us -> none  [the longest x4 89.3 us: shards(): jnp.einsum('fg,mgxy->mfxy', blending_matrix, centre, precision=HIGHEST)]
    reshape x8 -> x0, local copies, waits for them, and re-layouts: 190 us -> none  [the longest x1 83.5 us: shards(): returned.reshape(members, patch_count, mem_dev, levels, patch_cols)]
    pallas_call x0 -> x6, Pallas kernels: none -> 121 us  [call(): pl.pallas_call(kernel, out_shape=[jax.ShapeDtypeStruct(s, F32) for s in o...]
    transpose x2 -> x0, local copies, waits for them, and re-layouts: 85.8 us -> none  [the longest x1 45.6 us: shards(): returned.reshape(members, patch_count, mem_dev, levels, patch_cols)]
    slice x18 -> x1, local copies, waits for them, and re-layouts: 62.6 us -> 3.1 us  [shards(): x, head, tail = (ensemble, ensemble[:, :, :GY], ensemble[:, :, -GY:])]
    ppermute x8, waiting for transfers between devices: 161 us -> 193 us  [the longest x4 105 us: shards(): lax.ppermute(tail, 'region', [(i, (i + 1) % regions) for i in range(regio...]
    pallas_call x0 -> x7, local copies, waits for them, and re-layouts: none -> 14.3 us  [call(): pl.pallas_call(kernel, out_shape=[jax.ShapeDtypeStruct(s, F32) for s in o...]
    while x2 -> x0, local copies, waits for them, and re-layouts: 11.7 us -> none  [shards(): lax.map(analyse, (neighbourhood_tiles, obs_op, obs_value, obs_precision))]
  transfers between devices with their start and end apart: 9 -> 9, of which waited for: 9 -> 9; matrix products, arithmetic and copies ran while one was open for 6% -> 4% of each run, Pallas kernels for 0% -> 0%
where the time goes in v1:
time: 498 us; the launch traced here: 497 us
  waiting for transfers between devices  246 us (49%)
  Pallas kernels  121 us (24%)
  blocking collectives  62 us (12%)
  local copies, waits for them, and re-layouts  44.1 us (9%)
  starting transfers between devices  23.7 us (5%)
    pallas_call x6, Pallas kernels, call(): pl.pallas_call(kernel, out_shape=[jax.ShapeDtypeStruct(s, F32) for s in o...  121 us
    ppermute x4, waiting for transfers between devices, shards(): lax.ppermute(tail, 'region', [(i, (i + 1) % regions) for i in range(regio...  105 us
    ppermute x4, waiting for transfers between devices, shards(): lax.ppermute(head, 'region', [((i + 1) % regions, i) for i in range(regio...  87.8 us
    all_to_all x1, blocking collectives, shards(): lax.all_to_all(back, 'member', split_axis=0, concat_axis=0, tiled=True)  62 us
    all_to_all x1, waiting for transfers between devices, shards(): got = lax.all_to_all(out, 'member', split_axis=0, concat_axis=0, tiled=True)  53.3 us
    pallas_call x7, local copies, waits for them, and re-layouts, call(): pl.pallas_call(kernel, out_shape=[jax.ShapeDtypeStruct(s, F32) for s in o...  14.3 us
    ppermute x4, starting transfers between devices, shards(): lax.ppermute(head, 'region', [((i + 1) % regions, i) for i in range(regio...  13.4 us
  transfers between devices with their start and end apart: 9, of which 9 were waited for; matrix products, arithmetic and copies ran while one was open for 4% of the time, Pallas kernels for 0%

profile of v1, /device:TPU:0, one launch (start us, length us, event | category | flops | bytes accessed | tf_op | source)
XLA Modules:
  0.0 497.4 jit_solution(7879716077313215063)
XLA Ops:
  0.0 3.1 fusion
  8.2 5.3 %copy.33.x_ref = f32[32,76,512]{2,1,0:T(8,128)} copy(f32[32,76,512]{2,0,1:T(8,128)S(1)} %copy-done) | data formatting | bytes 9961472 | tf_op args[0]
  15.1 21.7 %collective-permute-done = f32[32,76,128]{2,0,1:T(8,128)} collective-permute-done((f32[32,76,128]{2,0,1:T(8,128)}, f32[32,76,128]{2,0,1:T(8,128)}, u32[]{:S(2)}, u32[]{:S(2)}) %collective-permute-start) | collective-permute-done | bytes 1245216 | tf_op jit(solution)/shard_map/ppermute | solution.py:270
  36.7 3.1 copy.34.up_ref
  39.8 21.9 %collective-permute-done.1 = f32[32,76,128]{2,0,1:T(8,128)S(1)} collective-permute-done((f32[32,76,128]{2,0,1:T(8,128)S(1)}, f32[32,76,128]{2,0,1:T(8,128)S(1)}, u32[]{:S(2)}, u32[]{:S(2)}) %collective-permute-start.1) | collective-permute-done | bytes 1245216 | tf_op jit(solution)/shard_map/ppermute | solution.py:271
  63.4 12.7 %shard_map.64 = (f32[32,76,512]{2,1,0:T(8,128)}, f32[32,76,128]{2,1,0:T(8,128)}, f32[32,76,128]{2,1,0:T(8,128)}) custom-call(f32[32,76,512]{2,1,0:T(8,128)} %copy.33.x_ref, f32[32,76,128]{2,1,0:T(8,128)} %copy.34.up_ref, f32[32,76,128]{2,1,0:T(8,128)} %copy.35.down_ref, f32[80,240]{1,0:T(8,128)} %copy.36.blend_ref, f32[76,1]{1,0:T(8,128)} %copy.37.rate_ref), custom_call_target="tpu_custom_call" | custom-call | tf_op jit(solution)/shard_map/pallas_call | solution.py:248
  79.7 4.4 collective-permute-start.3
  84.1 27.8 %collective-permute-done.2 = f32[32,76,128]{2,0,1:T(8,128)S(1)} collective-permute-done((f32[32,76,128]{2,0,1:T(8,128)S(1)}, f32[32,76,128]{2,0,1:T(8,128)S(1)}, u32[]{:S(2)}, u32[]{:S(2)}) %collective-permute-start.2) | collective-permute-done | bytes 1245216 | tf_op jit(solution)/shard_map/ppermute | solution.py:270
  113.7 21.2 %collective-permute-done.3 = f32[32,76,128]{2,0,1:T(8,128)S(1)} collective-permute-done((f32[32,76,128]{2,0,1:T(8,128)S(1)}, f32[32,76,128]{2,0,1:T(8,128)S(1)}, u32[]{:S(2)}, u32[]{:S(2)}) %collective-permute-start.3) | collective-permute-done | bytes 1245216 | tf_op jit(solution)/shard_map/ppermute | solution.py:271
  136.7 12.7 %shard_map.65 = (f32[32,76,512]{2,1,0:T(8,128)}, f32[32,76,128]{2,1,0:T(8,128)}, f32[32,76,128]{2,1,0:T(8,128)}) custom-call(f32[32,76,512]{2,1,0:T(8,128)} %get-tuple-element.14.x_ref, f32[32,76,128]{2,1,0:T(8,128)} %copy.40.up_ref, f32[32,76,128]{2,1,0:T(8,128)} %copy.41.down_ref, f32[80,240]{1,0:T(8,128)} %copy.36.blend_ref, f32[76,1]{1,0:T(8,128)} %copy.37.rate_ref), custom_call_target="tpu_custom_call" | custom-call | tf_op jit(solution)/shard_map/pallas_call | solution.py:248
  152.2 3.3 collective-permute-start.5
  155.5 27.8 %collective-permute-done.4 = f32[32,76,128]{2,0,1:T(8,128)S(1)} collective-permute-done((f32[32,76,128]{2,0,1:T(8,128)S(1)}, f32[32,76,128]{2,0,1:T(8,128)S(1)}, u32[]{:S(2)}, u32[]{:S(2)}) %collective-permute-start.4) | collective-permute-done | bytes 1245216 | tf_op jit(solution)/shard_map/ppermute | solution.py:270
  185.1 22.9 %collective-permute-done.5 = f32[32,76,128]{2,0,1:T(8,128)S(1)} collective-permute-done((f32[32,76,128]{2,0,1:T(8,128)S(1)}, f32[32,76,128]{2,0,1:T(8,128)S(1)}, u32[]{:S(2)}, u32[]{:S(2)}) %collective-permute-start.5) | collective-permute-done | bytes 1245216 | tf_op jit(solution)/shard_map/ppermute | solution.py:271
  209.7 12.7 %shard_map.66 = (f32[32,76,512]{2,1,0:T(8,128)}, f32[32,76,128]{2,1,0:T(8,128)}, f32[32,76,128]{2,1,0:T(8,128)}) custom-call(f32[32,76,512]{2,1,0:T(8,128)} %get-tuple-element.17.x_ref, f32[32,76,128]{2,1,0:T(8,128)} %copy.46.up_ref, f32[32,76,128]{2,1,0:T(8,128)} %copy.47.down_ref, f32[80,240]{1,0:T(8,128)} %copy.36.blend_ref, f32[76,1]{1,0:T(8,128)} %copy.37.rate_ref), custom_call_target="tpu_custom_call" | custom-call | tf_op jit(solution)/shard_map/pallas_call | solution.py:248
  225.2 3.6 collective-permute-start.7
  228.7 27.8 %collective-permute-done.6 = f32[32,76,128]{2,0,1:T(8,128)S(1)} collective-permute-done((f32[32,76,128]{2,0,1:T(8,128)S(1)}, f32[32,76,128]{2,0,1:T(8,128)S(1)}, u32[]{:S(2)}, u32[]{:S(2)}) %collective-permute-start.6) | collective-permute-done | bytes 1245216 | tf_op jit(solution)/shard_map/ppermute | solution.py:270
  258.4 21.8 %collective-permute-done.7 = f32[32,76,128]{2,0,1:T(8,128)S(1)} collective-permute-done((f32[32,76,128]{2,0,1:T(8,128)S(1)}, f32[32,76,128]{2,0,1:T(8,128)S(1)}, u32[]{:S(2)}, u32[]{:S(2)}) %collective-permute-start.7) | collective-permute-done | bytes 1245216 | tf_op jit(solution)/shard_map/ppermute | solution.py:271
  282.0 13.0 %shard_map.67 = f32[8,1216,128]{2,1,0:T(8,128)} custom-call(f32[32,76,512]{2,1,0:T(8,128)} %get-tuple-element.20.x_ref, f32[32,76,128]{2,1,0:T(8,128)} %copy.52.up_ref, f32[32,76,128]{2,1,0:T(8,128)} %copy.53.down_ref, f32[80,240]{1,0:T(8,128)} %copy.36.blend_ref, f32[76,1]{1,0:T(8,128)} %copy.37.rate_ref), custom_call_target="tpu_custom_call" | custom-call | tf_op jit(solution)/shard_map/pallas_call | solution.py:248
  295.0 4.8 all-to-all-start
  304.0 53.3 %all-to-all-done.x_ref = f32[8,1216,128]{2,1,0:T(8,128)} async-done(((f32[8,1216,128]{2,1,0:T(8,128)}), f32[8,1216,128]{2,1,0:T(8,128)}, u32[]{:S(2)}, u32[]{:S(2)}) %all-to-all-start) | async-done | bytes 4980768 | tf_op jit(solution)/shard_map/all_to_all | solution.py:278
  357.3 62.0 %shard_map.68 = f32[8,1216,128]{2,1,0:T(8,128)} custom-call(f32[8,1216,128]{2,1,0:T(8,128)} %all-to-all-done.x_ref, f32[8,128,608]{2,1,0:T(8,128)} %copy.56.op_ref, f32[8,128,1]{2,1,0:T(8,128)} %copy.57.val_ref, f32[8,128,1]{2,1,0:T(8,128)} %copy.58.prec_ref), custom_call_target="tpu_custom_call" | custom-call | tf_op jit(solution)/shard_map/pallas_call | solution.py:248
  419.3 62.0 %all_to_all.10.x_ref = f32[8,1216,128]{2,1,0:T(8,128)} all-to-all(f32[8,1216,128]{2,1,0:T(8,128)} %shard_map.68), channel_id=1, replica_groups=mesh['member'=8,'region'=4] {'member'}, dimensions={0} | all-to-all | bytes 9961472 | tf_op jit(solution)/shard_map/all_to_all | solution.py:290
  481.3 8.4 %shard_map.69 = f32[32,76,512]{2,1,0:T(8,128)} custom-call(f32[8,1216,128]{2,1,0:T(8,128)} %all_to_all.10.x_ref), custom_call_target="tpu_custom_call" | custom-call | tf_op jit(solution)/shard_map/pallas_call | solution.py:248
  489.8 7.6 %copy.59 = f32[32,76,512]{2,0,1:T(8,128)} copy(f32[32,76,512]{2,1,0:T(8,128)} %shard_map.69) | data formatting | bytes 9961472 | tf_op jit(solution)/shard_map/pallas_call | solution.py:248
  (44 shorter events, 32.6 us)
Async XLA Ops:
  0.0 8.2 %copy-start = (f32[32,76,512]{2,0,1:T(8,128)S(1)}, f32[32,76,512]{2,0,1:T(8,128)}, u32[]{:S(2)}) copy-start(f32[32,76,512]{2,0,1:T(8,128)} %param.6) | copy-start | bytes 14942212
  3.1 33.6 %collective-permute-start = (f32[32,76,128]{2,0,1:T(8,128)}, f32[32,76,128]{2,0,1:T(8,128)}, u32[]{:S(2)}, u32[]{:S(2)}) collective-permute-start(f32[32,76,128]{2,0,1:T(8,128)} %get-tuple-element.24), channel_id=1, source_target_pairs={{0,1},{1,2},{2,3},{3,0},{4,5},{5,6},{6,7},{7,4},{8,9},{9,10},{10,1... | collective-permute-start | bytes 3735560 | tf_op jit(solution)/shard_map/ppermute | solution.py:270
  6.1 7.3 %copy-start.5 = (f32[76,76]{1,0:T(8,128)S(1)}, f32[76,76]{1,0:T(8,128)}, u32[]{:S(2)}) copy-start(f32[76,76]{1,0:T(8,128)} %param.7) | copy-start | bytes 69316
  6.1 8.2 %copy-start.8 = (f32[76]{0:T(128)S(1)}, f32[76]{0:T(128)}, u32[]{:S(2)}) copy-start(f32[76]{0:T(128)} %param.8) | copy-start | bytes 916
  6.1 55.5 %collective-permute-start.1 = (f32[32,76,128]{2,0,1:T(8,128)S(1)}, f32[32,76,128]{2,0,1:T(8,128)S(1)}, u32[]{:S(2)}, u32[]{:S(2)}) collective-permute-start(f32[32,76,128]{2,0,1:T(8,128)S(1)} %get-tuple-element.23), channel_id=1, source_target_pairs={{1,0},{2,1},{3,2},{0,3},{5,4},{6,5},{7,6},{4,7},{9,8},{10,9},{11,1... | collective-permute-start | bytes 3735560 | tf_op jit(solution)/shard_map/ppermute | solution.py:271
  76.1 3.2 copy-start.2
  77.9 34.0 %collective-permute-start.2 = (f32[32,76,128]{2,0,1:T(8,128)S(1)}, f32[32,76,128]{2,0,1:T(8,128)S(1)}, u32[]{:S(2)}, u32[]{:S(2)}) collective-permute-start(f32[32,76,128]{2,0,1:T(8,128)S(1)} %copy.38), channel_id=1, source_target_pairs={{0,1},{1,2},{2,3},{3,0},{4,5},{5,6},{6,7},{7,4},{8,9},{9,10},{10,1... | collective-permute-start | bytes 3735560 | tf_op jit(solution)/shard_map/ppermute | solution.py:270
  79.7 55.2 %collective-permute-start.3 = (f32[32,76,128]{2,0,1:T(8,128)S(1)}, f32[32,76,128]{2,0,1:T(8,128)S(1)}, u32[]{:S(2)}, u32[]{:S(2)}) collective-permute-start(f32[32,76,128]{2,0,1:T(8,128)S(1)} %copy.39), channel_id=1, source_target_pairs={{1,0},{2,1},{3,2},{0,3},{5,4},{6,5},{7,6},{4,7},{9,8},{10,9},{11,1... | collective-permute-start | bytes 3735560 | tf_op jit(solution)/shard_map/ppermute | solution.py:271
  149.4 2.4 copy-start.3
  151.2 32.1 %collective-permute-start.4 = (f32[32,76,128]{2,0,1:T(8,128)S(1)}, f32[32,76,128]{2,0,1:T(8,128)S(1)}, u32[]{:S(2)}, u32[]{:S(2)}) collective-permute-start(f32[32,76,128]{2,0,1:T(8,128)S(1)} %copy.44), channel_id=1, source_target_pairs={{0,1},{1,2},{2,3},{3,0},{4,5},{5,6},{6,7},{7,4},{8,9},{9,10},{10,1... | collective-permute-start | bytes 3735560 | tf_op jit(solution)/shard_map/ppermute | solution.py:270
  152.2 55.8 %collective-permute-start.5 = (f32[32,76,128]{2,0,1:T(8,128)S(1)}, f32[32,76,128]{2,0,1:T(8,128)S(1)}, u32[]{:S(2)}, u32[]{:S(2)}) collective-permute-start(f32[32,76,128]{2,0,1:T(8,128)S(1)} %copy.45), channel_id=1, source_target_pairs={{1,0},{2,1},{3,2},{0,3},{5,4},{6,5},{7,6},{4,7},{9,8},{10,9},{11,1... | collective-permute-start | bytes 3735560 | tf_op jit(solution)/shard_map/ppermute | solution.py:271
  222.4 2.4 copy-start.4
  224.2 32.4 %collective-permute-start.6 = (f32[32,76,128]{2,0,1:T(8,128)S(1)}, f32[32,76,128]{2,0,1:T(8,128)S(1)}, u32[]{:S(2)}, u32[]{:S(2)}) collective-permute-start(f32[32,76,128]{2,0,1:T(8,128)S(1)} %copy.50), channel_id=1, source_target_pairs={{0,1},{1,2},{2,3},{3,0},{4,5},{5,6},{6,7},{7,4},{8,9},{9,10},{10,1... | collective-permute-start | bytes 3735560 | tf_op jit(solution)/shard_map/ppermute | solution.py:270
  225.2 55.1 %collective-permute-start.7 = (f32[32,76,128]{2,0,1:T(8,128)S(1)}, f32[32,76,128]{2,0,1:T(8,128)S(1)}, u32[]{:S(2)}, u32[]{:S(2)}) collective-permute-start(f32[32,76,128]{2,0,1:T(8,128)S(1)} %copy.51), channel_id=1, source_target_pairs={{1,0},{2,1},{3,2},{0,3},{5,4},{6,5},{7,6},{4,7},{9,8},{10,9},{11,1... | collective-permute-start | bytes 3735560 | tf_op jit(solution)/shard_map/ppermute | solution.py:271
  295.0 4.8 copy-start.1
  295.0 62.3 %all-to-all-start = ((f32[8,1216,128]{2,1,0:T(8,128)}), f32[8,1216,128]{2,1,0:T(8,128)}, u32[]{:S(2)}, u32[]{:S(2)}) async-start(f32[8,1216,128]{2,1,0:T(8,128)} %shard_map.67), calls=%async_computation | async-start | bytes 9961472 | tf_op jit(solution)/shard_map/all_to_all | solution.py:278
  299.8 2.1 copy-start.6
  299.8 3.2 copy-start.7

commit v2 on v1

--- a/solution.py
+++ b/solution.py
@@ -56,14 +56,14 @@
     return jnp.where(lane < 2 * padded, hi.astype(F32), lo.astype(F32)).astype(BF16)
 
 
-def advance(x, up, down, mix, rate):
+def advance(parts, up, down, mix, rate):
+    x = jnp.concatenate(parts, 1)
     levels = x.shape[0]
     padded = mix.shape[0]
     full = jnp.concatenate([x, jnp.zeros((padded - levels, x.shape[1]), F32)], 0)
     hi, lo = split2(full)
     coupled = mm(mix, jnp.concatenate([hi, lo, hi], 0))[:levels]
     rows = x.shape[1] // GY
-    parts = [x[:, r * GY:(r + 1) * GY] for r in range(rows)]
     ext = [up] + parts + [down]
     out = []
     for r in range(rows):
@@ -73,52 +73,112 @@
     return out
 
 
-def step_kernel(x_ref, up_ref, down_ref, blend_ref, rate_ref, o_ref, head_ref, tail_ref):
-    levels = x_ref.shape[1]
-    mix = mixing(blend_ref, levels)
-    rate = rate_ref[...]
-
-    @pl.loop(0, x_ref.shape[0])
-    def _(m):
-        new = advance(x_ref[m], up_ref[m], down_ref[m], mix, rate)
-        for r, part in enumerate(new):
-            o_ref[m, :, r * GY:(r + 1) * GY] = part
-        head_ref[m] = new[0]
-        tail_ref[m] = new[-1]
-
-
 def rows_of(i, levels, stride):
-    return pl.ds(i, levels) if stride == 1 else pl.ds(i, levels, stride=stride)
-
-
-def last_kernel(x_ref, up_ref, down_ref, blend_ref, rate_ref, o_ref):
-    mem, levels, cols = x_ref.shape
-    rows = cols // GY
-    pack = o_ref.shape[0] // rows
+    return pl.ds(0, levels) if stride == 1 else pl.ds(i, levels, stride=stride)
+
+
+def groups_of(group):
+    count = max(1, group // 8)
+    return count, group // count
+
+
+def others(axis):
+    count = lax.axis_size(axis)
+    me = lax.axis_index(axis)
+    return me, [lax.rem(me + j, count) for j in range(1, count)]
+
+
+def forecast_kernel(ens_ref, blend_ref, rate_ref, o_ref, x_ref, up_ref, down_ref, pack_ref,
+                    load_sem, halo_send, halo_recv, part_send, part_recv, own_sem):
+    rows, count, pack, size, levels, _ = x_ref.shape
     width = GY // pack
-    group = mem // pack
+    me, peers = others("member")
+    regions = lax.axis_size("region")
+    here = lax.axis_index("region")
+    above = lax.rem(here + 1, regions)
+    below = lax.rem(here + regions - 1, regions)
+
+    loads = {}
+    for g in range(count):
+        for r in range(rows):
+            for h in range(pack):
+                first = (h * count + g) * size
+                loads[g, r, h] = pltpu.make_async_copy(
+                    ens_ref.at[pl.ds(first, size), :, pl.ds(r * GY, GY)],
+                    x_ref.at[r, g, h], load_sem.at[g, r, h])
+                loads[g, r, h].start()
+
+    barrier = pltpu.get_barrier_semaphore()
+    for other in peers:
+        pl.semaphore_signal(barrier, inc=1, device_id={"member": other},
+                            device_id_type=pl.DeviceIdType.MESH)
+    for other in (above, below):
+        pl.semaphore_signal(barrier, inc=1, device_id={"region": other},
+                            device_id_type=pl.DeviceIdType.MESH)
+    pl.semaphore_wait(barrier, len(peers) + 2)
+
+    def halos(k, g):
+        return [
+            pltpu.make_async_remote_copy(
+                src_ref=x_ref.at[r, g], dst_ref=ref.at[k, g],
+                send_sem=halo_send.at[side, k, g], recv_sem=halo_recv.at[side, k, g],
+                device_id={"region": other}, device_id_type=pl.DeviceIdType.MESH)
+            for side, (r, ref, other) in enumerate(
+                ((rows - 1, up_ref, above), (0, down_ref, below)))
+        ]
+
+    def part(g, j):
+        return pltpu.make_async_remote_copy(
+            src_ref=pack_ref.at[peers[j], g], dst_ref=o_ref.at[me, g],
+            send_sem=part_send.at[g, j], recv_sem=part_recv.at[g, j],
+            device_id={"member": peers[j]}, device_id_type=pl.DeviceIdType.MESH)
+
     mix = mixing(blend_ref, levels)
     rate = rate_ref[...]
     place = lax.broadcasted_iota(jnp.int32, (levels, GY), 1) // width
 
-    def body(i):
-        news = []
-        for h in range(pack):
-            m = h * group + i
-            news.append(advance(x_ref[m], up_ref[m], down_ref[m], mix, rate))
+    for g in range(count):
         for r in range(rows):
-            for c in range(pack):
-                value = news[c][r]
+            for h in range(pack):
+                loads[g, r, h].wait()
+        for copy in halos(0, g):
+            copy.start()
+    for k in range(NSTEP):
+        for g in range(count):
+            for copy in halos(k, g):
+                copy.wait()
+
+            @pl.loop(0, size)
+            def _(i):
+                news = []
                 for h in range(pack):
-                    if h != c:
-                        moved = pltpu.roll(news[h][r], (h - c) * width % GY, 1)
-                        value = jnp.where(place == h, moved, value)
-                o_ref[r * pack + c, rows_of(i, levels, group), :] = value
-
-    if group == 1:
-        body(0)
-    else:
-        pl.loop(0, group)(body)
+                    new = advance([x_ref[r, g, h, i] for r in range(rows)],
+                                  up_ref[k, g, h, i], down_ref[k, g, h, i], mix, rate)
+                    news.append(new)
+                    if k < NSTEP - 1:
+                        for r in range(rows):
+                            x_ref[r, g, h, i] = new[r]
+                if k == NSTEP - 1:
+                    for r in range(rows):
+                        for c in range(pack):
+                            value = news[c][r]
+                            for h in range(pack):
+                                if h != c:
+                                    moved = pltpu.roll(news[h][r], (h - c) * width % GY, 1)
+                                    value = jnp.where(place == h, moved, value)
+                            pack_ref[r * pack + c, g, rows_of(i, levels, size), :] = value
+
+            if k < NSTEP - 1:
+                for copy in halos(k + 1, g):
+                    copy.start()
+            else:
+                for j in range(len(peers)):
+                    part(g, j).start()
+                pltpu.make_async_copy(pack_ref.at[me, g], o_ref.at[me, g], own_sem.at[g]).start()
+    for g in range(count):
+        for j in range(len(peers)):
+            part(g, j).wait()
+        pltpu.make_async_copy(pack_ref.at[me, g], o_ref.at[me, g], own_sem.at[g]).wait()
 
 
 def unpack_kernel(x_ref, o_ref):
@@ -126,46 +186,45 @@
     rows = cols // GY
     pack = x_ref.shape[0] // rows
     width = GY // pack
-    group = mem // pack
+    count, size = groups_of(mem // pack)
     place = lax.broadcasted_iota(jnp.int32, (levels, GY), 1) // width
 
-    def body(i):
-        for r in range(rows):
-            got = [x_ref[r * pack + c, rows_of(i, levels, group), :] for c in range(pack)]
-            for h in range(pack):
-                value = got[h]
-                for c in range(pack):
-                    if c != h:
-                        value = jnp.where(place == c, pltpu.roll(got[c], (c - h) * width % GY, 1), value)
-                o_ref[h * group + i, :, r * GY:(r + 1) * GY] = value
-
-    if group == 1:
-        body(0)
-    else:
-        pl.loop(0, group)(body)
+    for g in range(count):
+        @pl.loop(0, size)
+        def _(i):
+            for r in range(rows):
+                got = [x_ref[r * pack + c, g, rows_of(i, levels, size), :] for c in range(pack)]
+                for h in range(pack):
+                    value = got[h]
+                    for c in range(pack):
+                        if c != h:
+                            value = jnp.where(place == c, pltpu.roll(got[c], (c - h) * width % GY, 1), value)
+                    o_ref[(h * count + g) * size + i, :, r * GY:(r + 1) * GY] = value
 
 
 def analysis_kernel(levels, x_ref, op_ref, val_ref, prec_ref, o_ref,
                     xt_ref, mean_ref, u_ref, v_ref, state_ref, scal_ref):
-    sources, packed, _ = x_ref.shape
-    group = packed // levels
+    sources, count, packed, _ = x_ref.shape
+    size = packed // levels
     patches, nobs, entries = op_ref.shape
     cells = entries // levels
     ens = xt_ref.shape[2]
     width = patches * cells
     pack = GY // width
-    half = sources * group
+    share = sources * size
+    half = count * share
     a = ens - 1.0
     eye = (lax.broadcasted_iota(jnp.int32, (nobs, nobs), 0)
            == lax.broadcasted_iota(jnp.int32, (nobs, nobs), 1)).astype(F32)
 
     @pl.loop(0, levels)
     def _(f):
-        if group == 1:
-            x = x_ref[:, f, :]
+        if size == 1:
+            x = [x_ref[:, g, f, :] for g in range(count)]
         else:
-            x = x_ref[:, pl.ds(pl.multiple_of(f * group, group), group), :].reshape(half, GY)
-        t = x.T
+            x = [x_ref[:, g, pl.ds(pl.multiple_of(f * size, size), size), :].reshape(share, GY)
+                 for g in range(count)]
+        t = jnp.concatenate(x, 0).T
         for h in range(pack):
             for p in range(patches):
                 xt_ref[p, pl.ds(pl.multiple_of(f * cells, cells), cells), h * half:(h + 1) * half] = (
@@ -237,18 +296,20 @@
         t = jnp.concatenate([
             xt_ref[p, pl.ds(pl.multiple_of(f * cells, cells), cells), h * half:(h + 1) * half]
             for h in range(pack) for p in range(patches)], 0).T
-        if group == 1:
-            o_ref[:, f, :] = t
-        else:
-            o_ref[:, pl.ds(pl.multiple_of(f * group, group), group), :] = t.reshape(
-                sources, group, GY)
-
-
-def call(kernel, outs, args, scratch=(), params=PARAMS):
+        for g in range(count):
+            mine = t[g * share:(g + 1) * share]
+            if size == 1:
+                o_ref[:, g, f, :] = mine
+            else:
+                o_ref[:, g, pl.ds(pl.multiple_of(f * size, size), size), :] = mine.reshape(
+                    sources, size, GY)
+
+
+def call(kernel, outs, args, scratch=(), params=PARAMS, specs=None):
     return pl.pallas_call(
         kernel,
         out_shape=[jax.ShapeDtypeStruct(s, F32) for s in outs],
-        in_specs=[VMEM] * len(args),
+        in_specs=specs or [VMEM] * len(args),
         out_specs=[VMEM] * len(outs),
         scratch_shapes=list(scratch),
         compiler_params=params,
@@ -258,24 +319,32 @@
 def shards(ensemble, blending_matrix, lateral_spreading, obs_op, obs_value, obs_precision):
     mem, levels, cols = ensemble.shape
     members = lax.axis_size("member")
-    regions = lax.axis_size("region")
     patches, nobs, entries = obs_op.shape
     ens = mem * members
+    rows = cols // GY
     pack = GY * members // cols
+    count, size = groups_of(mem // pack)
     padded = -(-levels // 16) * 16
     blend = jnp.tile(jnp.pad(blending_matrix, ((0, padded - levels),) * 2), (1, 3))
     rate = lateral_spreading[:, None]
-    x, head, tail = ensemble, ensemble[:, :, :GY], ensemble[:, :, -GY:]
-    for step in range(NSTEP):
-        up = lax.ppermute(tail, "region", [(i, (i + 1) % regions) for i in range(regions)])
-        down = lax.ppermute(head, "region", [((i + 1) % regions, i) for i in range(regions)])
-        args = (x, up, down, blend, rate)
-        if step < NSTEP - 1:
-            side = (mem, levels, GY)
-            x, head, tail = call(step_kernel, [x.shape, side, side], args)
-    packed = (members, levels * mem // pack, GY)
-    out, = call(last_kernel, [packed], args)
-    got = lax.all_to_all(out, "member", split_axis=0, concat_axis=0, tiled=True)
+    packed = (members, count, levels * size, GY)
+    dma = pltpu.SemaphoreType.DMA
+    got, = call(
+        forecast_kernel, [packed], (ensemble, blend, rate),
+        [
+            pltpu.VMEM((rows, count, pack, size, levels, GY), F32),
+            pltpu.VMEM((NSTEP, count, pack, size, levels, GY), F32),
+            pltpu.VMEM((NSTEP, count, pack, size, levels, GY), F32),
+            pltpu.VMEM(packed, F32),
+            dma((count, rows, pack)),
+            dma((2, NSTEP, count)),
+            dma((2, NSTEP, count)),
+            dma((count, members - 1)),
+            dma((count, members - 1)),
+            dma((count,)),
+        ],
+        pltpu.CompilerParams(vmem_limit_bytes=56 * 2**20, collective_id=0, has_side_effects=True),
+        [pl.BlockSpec(memory_space=pl.ANY), VMEM, VMEM])
     back, = call(
         functools.partial(analysis_kernel, levels), [packed],
         (got, obs_op, obs_value[:, :, None], obs_precision[:, :, None]),

time: 498 us -> 407 us (0.82)
  waiting for transfers between devices: 246 us -> 0 us
  Pallas kernels: 121 us -> 323 us
  starting transfers between devices: 23.7 us -> 0 us
  local copies, waits for them, and re-layouts: 44.1 us -> 21.2 us
    pallas_call x6 -> x3, Pallas kernels: 121 us -> 323 us  [call(): pl.pallas_call(kernel, out_shape=[jax.ShapeDtypeStruct(s, F32) for s in o...]
    ppermute x8 -> x0, waiting for transfers between devices: 193 us -> none  [the longest x4 105 us: shards(): lax.ppermute(tail, 'region', [(i, (i + 1) % regions) for i in range(regio...]
    all_to_all x1 -> x0, waiting for transfers between devices: 53.3 us -> none  [shards(): got = lax.all_to_all(out, 'member', split_axis=0, concat_axis=0, tiled=True)]
    ppermute x8 -> x0, starting transfers between devices: 19 us -> none  [the longest x4 13.4 us: shards(): lax.ppermute(head, 'region', [((i + 1) % regions, i) for i in range(regio...]
    ppermute x8 -> x0, local copies, waits for them, and re-layouts: 15.6 us -> none  [the longest x4 8.46 us: shards(): lax.ppermute(tail, 'region', [(i, (i + 1) % regions) for i in range(regio...]
    pallas_call x7 -> x1, local copies, waits for them, and re-layouts: 14.3 us -> 7.64 us  [call(): pl.pallas_call(kernel, out_shape=[jax.ShapeDtypeStruct(s, F32) for s in o...]
  transfers between devices with their start and end apart: 9 -> 0, of which waited for: 9 -> 0; matrix products, arithmetic and copies ran while one was open for 4% -> 0% of each run, Pallas kernels for 0% -> 0%
where the time goes in v2:
time: 407 us
  Pallas kernels  323 us (79%)
  blocking collectives  62.3 us (15%)
  local copies, waits for them, and re-layouts  21.2 us (5%)
    pallas_call x3, Pallas kernels, call(): pl.pallas_call(kernel, out_shape=[jax.ShapeDtypeStruct(s, F32) for s in o...  323 us
    all_to_all x1, blocking collectives, shards(): lax.all_to_all(back, 'member', split_axis=0, concat_axis=0, tiled=True)  62.3 us
    unnamed x13, local copies, waits for them, and re-layouts  9.95 us

profile of v2, /device:TPU:0, one launch (start us, length us, event | category | flops | bytes accessed | tf_op | source)
XLA Modules:
  0.0 406.5 jit_solution(492615198815938027)
XLA Ops:
  0.0 0.0 copy-start.1
  0.0 0.0 copy-start.4
  0.0 0.0 copy-start
  0.0 7.8 %copy.12.ens_ref = f32[32,76,512]{2,1,0:T(8,128)} copy(f32[32,76,512]{2,0,1:T(8,128)} %param.6) | data formatting | bytes 9961472 | tf_op args[0]
  7.8 0.0 copy-done.1
  7.8 0.0 copy-start.2
  7.8 0.0 copy-start.3
  7.8 0.1 copy.19
  7.9 0.7 copy.13.blend_ref
  8.6 0.0 copy-done.4
  8.6 0.7 copy.14.rate_ref
  9.3 0.0 copy-done
  9.3 2.1 copy.15.op_ref
  11.4 0.0 copy-done.2
  11.4 1.1 copy.16.val_ref
  12.5 0.0 copy-done.3
  12.5 1.1 copy.17.prec_ref
  13.6 253.8 %shard_map.64.x_ref = f32[8,2,608,128]{3,2,1,0:T(8,128)} custom-call(f32[32,76,512]{2,1,0:T(8,128)} %copy.12.ens_ref, f32[80,240]{1,0:T(8,128)} %copy.13.blend_ref, f32[76,1]{1,0:T(8,128)} %copy.14.rate_ref), custom_call_target="tpu_custom_call" | custom-call | tf_op jit(solution)/shard_map/pallas_call | solution.py:309
  267.4 62.0 %shard_map.65 = f32[8,2,608,128]{3,2,1,0:T(8,128)} custom-call(f32[8,2,608,128]{3,2,1,0:T(8,128)} %shard_map.64.x_ref, f32[8,128,608]{2,1,0:T(8,128)} %copy.15.op_ref, f32[8,128,1]{2,1,0:T(8,128)} %copy.16.val_ref, f32[8,128,1]{2,1,0:T(8,128)} %copy.17.prec_ref), custom_call_target="tpu_custom_call" | custom-call | tf_op jit(solution)/shard_map/pallas_call | solution.py:309
  329.4 62.3 %all_to_all.5.x_ref = f32[8,2,608,128]{3,2,1,0:T(8,128)} all-to-all(f32[8,2,608,128]{3,2,1,0:T(8,128)} %shard_map.65), channel_id=1, replica_groups=mesh['member'=8,'region'=4] {'member'}, dimensions={0} | all-to-all | bytes 9961472 | tf_op jit(solution)/shard_map/all_to_all | solution.py:359
  391.7 7.2 %shard_map.66 = f32[32,76,512]{2,1,0:T(8,128)} custom-call(f32[8,2,608,128]{3,2,1,0:T(8,128)} %all_to_all.5.x_ref), custom_call_target="tpu_custom_call" | custom-call | tf_op jit(solution)/shard_map/pallas_call | solution.py:309
  398.9 7.6 %copy.18 = f32[32,76,512]{2,0,1:T(8,128)} copy(f32[32,76,512]{2,1,0:T(8,128)} %shard_map.66) | data formatting | bytes 9961472 | tf_op jit(solution)/shard_map/pallas_call | solution.py:309
  (2 shorter events, 0.0 us)
Async XLA Ops:
  0.0 7.8 %copy-start.1 = (f32[76,76]{1,0:T(8,128)S(1)}, f32[76,76]{1,0:T(8,128)}, u32[]{:S(2)}) copy-start(f32[76,76]{1,0:T(8,128)} %param.7) | copy-start | bytes 69316
  0.0 8.6 %copy-start.4 = (f32[76]{0:T(128)S(1)}, f32[76]{0:T(128)}, u32[]{:S(2)}) copy-start(f32[76]{0:T(128)} %param.8) | copy-start | bytes 916
  0.0 9.3 %copy-start = (f32[8,128,608]{1,2,0:T(8,128)S(1)}, f32[8,128,608]{1,2,0:T(8,128)}, u32[]{:S(2)}) copy-start(f32[8,128,608]{1,2,0:T(8,128)} %param.9) | copy-start | bytes 7471108
  7.8 3.7 copy-start.2
  7.8 4.7 %copy-start.3 = (f32[8,128]{1,0:T(8,128)S(1)}, f32[8,128]{1,0:T(8,128)}, u32[]{:S(2)}) copy-start(f32[8,128]{1,0:T(8,128)} %param.11) | copy-start | bytes 12292

commit v3 on v2

v3 whole, which is shorter than its diff:
```python
import functools
import math

import jax
import jax.numpy as jnp
from jax import lax
from jax.experimental import pallas as pl
from jax.experimental.pallas import tpu as pltpu
from jax.sharding import PartitionSpec as P

GY = 128
NSTEP = 4
ITERS = 12
HIGHEST = lax.Precision.HIGHEST
F32 = jnp.float32
BF16 = jnp.bfloat16
VMEM = pl.BlockSpec(memory_space=pltpu.VMEM)
PARAMS = pltpu.CompilerParams(vmem_limit_bytes=56 * 2**20)


def mm(a, b):
    return jnp.dot(a, b, preferred_element_type=F32)


def split2(x):
    hi = x.astype(BF16)
    return hi, (x - hi.astype(F32)).astype(BF16)


def split3(x):
    hi = x.astype(BF16)
    rest = x - hi.astype(F32)
    mid = rest.astype(BF16)
    return hi, mid, (rest - mid.astype(F32)).astype(BF16)


def dot3(a, b):
    a0, a1 = split2(a)
    b0, b1 = split2(b)
    return mm(a0, b0) + (mm(a0, b1) + mm(a1, b0))


def dot6(a, b):
    a0, a1, a2 = split3(a)
    b0, b1, b2 = split3(b)
    left = jnp.concatenate([a0, a1], 1)
    low = mm(jnp.concatenate([a0, a2], 1), jnp.concatenate([b2, b0], 0))
    low = low + mm(left, jnp.concatenate([b1, b0], 0))
    return low + mm(left, jnp.concatenate([b0, b1], 0))


def mixing(blend_ref, levels):
    padded = blend_ref.shape[0]
    hi, lo = split2(blend_ref[...])
    lane = lax.broadcasted_iota(jnp.int32, blend_ref.shape, 1)
    return jnp.where(lane < 2 * padded, hi.astype(F32), lo.astype(F32)).astype(BF16)


def advance(parts, mix, rate):
    x = jnp.concatenate(parts, 1)
    levels = x.shape[0]
    padded = mix.shape[0]
    full = jnp.concatenate([x, jnp.zeros((padded - levels, x.shape[1]), F32)], 0)
    hi, lo = split2(full)
    coupled = mm(mix, jnp.concatenate([hi, lo, hi], 0))[:levels]
    rows = len(parts)
    out = []
    for r in range(rows):
        c = parts[r]
        lap = pltpu.roll(c, 1, 1) + pltpu.roll(c, GY - 1, 1) - 4.0 * c
        if r:
            lap = lap + parts[r - 1]
        if r < rows - 1:
            lap = lap + parts[r + 1]
        out.append(c + rate * lap + 0.3 * jnp.tanh(coupled[:, r * GY:(r + 1) * GY]))
    return out


def rows_of(i, levels, stride):
    return pl.ds(0, levels) if stride == 1 else pl.ds(i, levels, stride=stride)


def groups_of(group):
    count = max(1, group // 8)
    return count, group // count


def others(axis):
    count = lax.axis_size(axis)
    me = lax.axis_index(axis)
    return me, [lax.rem(me + j, count) for j in range(1, count)]


def swap_blocks(tiles):
    count = len(tiles)
    width = GY // count
    block = lax.broadcasted_iota(jnp.int32, tiles[0].shape, 1) // width
    bit = 1
    while bit < count:
        low = lax.rem(block // bit, 2) == 0
        out = list(tiles)
        for k in range(count):
            if not k & bit:
                a, b = tiles[k], tiles[k | bit]
                out[k] = jnp.where(low, a, pltpu.roll(b, bit * width, 1))
                out[k | bit] = jnp.where(low, pltpu.roll(a, GY - bit * width, 1), b)
        tiles = out
        bit *= 2
    return tiles


def each(total, unroll, body):
    trips = total // unroll
    if trips:
        @pl.loop(0, trips)
        def _(i):
            for d in range(unroll):
                body(i * unroll + d)
    for d in range(trips * unroll, total):
        body(d)


def tile_rows(f, size):
    return pl.ds(f, 1) if size == 1 else pl.ds(pl.multiple_of(f * size, size), size)


def forecast_kernel(ens_ref, blend_ref, rate_ref, o_ref, x_ref, up_ref, down_ref, pack_ref, rate_rows,
                    halo_send, halo_recv, part_send, part_recv, own_sem):
    _, rows, count, pack, packed, _ = x_ref.shape
    levels = ens_ref.shape[0]
    size = packed // levels
    members = lax.axis_size("member")
    me, peers = others("member")
    regions = lax.axis_size("region")
    here = lax.axis_index("region")
    above = lax.rem(here + 1, regions)
    below = lax.rem(here + regions - 1, regions)

    barrier = pltpu.get_barrier_semaphore()
    for other in peers:
        pl.semaphore_signal(barrier, inc=1, device_id={"member": other},
                            device_id_type=pl.DeviceIdType.MESH)
    for other in (above, below):
        pl.semaphore_signal(barrier, inc=1, device_id={"region": other},
                            device_id_type=pl.DeviceIdType.MESH)

    def halos(k, g):
        return [
            pltpu.make_async_remote_copy(
                src_ref=x_ref.at[k % 2, r, g], dst_ref=ref.at[k, g],
                send_sem=halo_send.at[side, k, g], recv_sem=halo_recv.at[side, k, g],
                device_id={"region": other}, device_id_type=pl.DeviceIdType.MESH)
            for side, (r, ref, other) in enumerate(
                ((rows - 1, up_ref, above), (0, down_ref, below)))
        ]

    def part(g, d):
        return pltpu.make_async_remote_copy(
            src_ref=pack_ref.at[d, g], dst_ref=o_ref.at[me, g],
            send_sem=part_send.at[g, d], recv_sem=part_recv.at[g, me],
            device_id={"member": d}, device_id_type=pl.DeviceIdType.MESH)

    def arrival(g, d):
        return pltpu.make_async_remote_copy(
            src_ref=pack_ref.at[d, g], dst_ref=o_ref.at[d, g],
            send_sem=part_send.at[g, d], recv_sem=part_recv.at[g, d],
            device_id={"member": d}, device_id_type=pl.DeviceIdType.MESH)

    def own(g):
        return pltpu.make_async_copy(pack_ref.at[me, g], o_ref.at[me, g], own_sem.at[g])

    mix = mixing(blend_ref, levels)
    rate = rate_ref[...]

    def load(g):
        def body(f):
            for r in range(rows):
                for h in range(pack):
                    first = (h * count + g) * size
                    x_ref[0, r, g, h, tile_rows(f, size), :] = (
                        ens_ref[f, first:first + size, r * GY:(r + 1) * GY])
        each(levels, 4, body)

    def inner(k, g):
        def body(i):
            place = rows_of(i, levels, size)
            for h in range(pack):
                new = advance([x_ref[k % 2, r, g, h, place, :] for r in range(rows)], mix, rate)
                for r in range(rows):
                    x_ref[(k + 1) % 2, r, g, h, place, :] = new[r]
        each(size, 2, body)

    def border(k, g):
        def body(f):
            place = tile_rows(f, size)
            factor = rate_rows[tile_rows(f, 8), :][:size]
            for h in range(pack):
                for r, ref in ((0, up_ref), (rows - 1, down_ref)):
                    x_ref[(k + 1) % 2, r, g, h, place, :] = (
                        x_ref[(k + 1) % 2, r, g, h, place, :] + factor * ref[k, g, h, place, :])
        each(levels, 4, body)

    def ship(g, chosen):
        def body(f):
            place = tile_rows(f, size)
            for r in chosen:
                tiles = swap_blocks([x_ref[NSTEP % 2, r, g, h, place, :] for h in range(pack)])
                for c in range(pack):
                    pack_ref[r * pack + c, g, place, :] = tiles[c]
        each(levels, 4, body)
        for r in chosen:
            for c in range(pack):
                d = r * pack + c

                @pl.when(me != d)
                def _():
                    part(g, d).start()

    for g in range(count):
        load(g)
        if g == 0:
            pl.semaphore_wait(barrier, len(peers) + 2)
        for copy in halos(0, g):
            copy.start()

    def body(f):
        rate_rows[tile_rows(f, 8), :] = jnp.broadcast_to(rate_ref[pl.ds(f, 1), :], (8, GY))
    each(levels, 4, body)
    for g in range(count):
        inner(0, g)
    for k in range(NSTEP):
        for g in range(count):
            for copy in halos(k, g):
                copy.wait()
            border(k, g)
            if k < NSTEP - 1:
                for copy in halos(k + 1, g):
                    copy.start()
                inner(k + 1, g)
                if k + 1 == NSTEP - 1:
                    ship(g, range(1, rows - 1))
            else:
                ship(g, sorted({0, rows - 1}))
                own(g).start()
    for g in range(count):
        for d in range(members):
            @pl.when(me != d)
            def _():
                part(g, d).wait_send()
                arrival(g, d).wait_recv()
        own(g).wait()


def unpack_kernel(chunk, x_ref, o_ref):
    sets, _, count, packed, _ = x_ref.shape
    mem, cols = o_ref.shape[2:]
    rows = cols // GY
    pack = x_ref.shape[1] // rows
    size = mem // (pack * count)

    def body(f):
        for g in range(count):
            for r in range(rows):
                tiles = swap_blocks([x_ref[c, r * pack + k, g, tile_rows(f, size), :]
                                     for k in range(pack) for c in range(sets)])
                for part in range(sets):
                    for h in range(pack):
                        first = (h * count + g) * size
                        o_ref[part, f, first:first + size, r * GY:(r + 1) * GY] = (
                            tiles[part * pack + h])
    each(chunk, 1, body)


def analysis_kernel(levels, x_ref, op_ref, val_ref, prec_ref, o_ref,
                    xt_ref, mean_ref, u_ref, v_ref, state_ref, scal_ref,
                    send_ref, send_sem, recv_sem, own_sem):
    sources, count, packed, _ = x_ref.shape
    size = packed // levels
    patches, entries, nobs = op_ref.shape
    sets = o_ref.shape[0]
    per_set = patches // sets
    chunk = levels // sets
    batches = 2
    per_batch = patches // batches
    me, peers = others("member")
    cells = entries // levels
    ens = xt_ref.shape[2]
    width = patches * cells
    pack = GY // width
    share = sources * size
    half = count * share
    a = ens - 1.0
    eye = (lax.broadcasted_iota(jnp.int32, (nobs, nobs), 0)
           == lax.broadcasted_iota(jnp.int32, (nobs, nobs), 1)).astype(F32)

    barrier = pltpu.get_barrier_semaphore()
    for other in peers:
        pl.semaphore_signal(barrier, inc=1, device_id={"member": other},
                            device_id_type=pl.DeviceIdType.MESH)

    def part(c, j):
        return pltpu.make_async_remote_copy(
            src_ref=send_ref.at[c, peers[j]], dst_ref=o_ref.at[c, me],
            send_sem=send_sem.at[c, j], recv_sem=recv_sem.at[c, j],
            device_id={"member": peers[j]}, device_id_type=pl.DeviceIdType.MESH)

    def own(c):
        return pltpu.make_async_copy(send_ref.at[c, me], o_ref.at[c, me], own_sem.at[c])

    def column(row):
        return jnp.sum(eye * row, axis=1, keepdims=True)

    def spread(f):
        if size == 1:
            x = [x_ref[:, g, f, :] for g in range(count)]
        else:
            x = [x_ref[:, g, tile_rows(f, size), :].reshape(share, GY) for g in range(count)]
        t = jnp.concatenate(x, 0).T
        for h in range(pack):
            for p in range(patches):
                xt_ref[p, tile_rows(f, cells), h * half:(h + 1) * half] = (
                    t[h * width + p * cells:h * width + (p + 1) * cells, :])
    each(levels, 4, spread)

    for b in range(batches):
        start = b * per_batch

        @pl.loop(start, start + per_batch)
        def _(p):
            x = xt_ref[p]
            mean = jnp.sum(x, axis=1, keepdims=True) * (1.0 / ens)
            e = x - mean
            xt_ref[p] = e
            mean_ref[p] = mean
            op = op_ref[p]
            obs_mean = jnp.sum(op * mean, axis=0, keepdims=True)
            root = jnp.sqrt(prec_ref[pl.ds(p, 1), :])
            u = dot3(op.T, e) * column(root)
            u_ref[p] = u
            v_ref[p] = root * (val_ref[pl.ds(p, 1), :] - obs_mean)
            gram = lax.dot_general(u, u, (((1,), (1,)), ((), ())), precision=HIGHEST,
                                   preferred_element_type=F32)
            trace = jnp.sum(u * u, keepdims=True).reshape(1, 1)
            square = jnp.sum(gram * gram, keepdims=True).reshape(1, 1)
            s = jnp.sqrt(a * a * ens + 2.0 * a * trace + square)
            alpha = a / s
            state_ref[p, :, 0:nobs] = alpha * eye + gram / s
            state_ref[p, :, nobs:2 * nobs] = eye
            state_ref[p, :, 2 * nobs:3 * nobs] = jnp.zeros_like(eye)
            scal_ref[p, 0:1, :] = jnp.broadcast_to(s, (1, GY))
            scal_ref[p, 1:2, :] = jnp.broadcast_to(alpha, (1, GY))
            scal_ref[p, 2:3, :] = jnp.ones((1, GY), F32)

        @pl.loop(0, ITERS)
        def _(k):
            firsts = {}
            for p in range(start, start + per_batch):
                state = state_ref[p]
                firsts[p] = dot6(state[:, nobs:2 * nobs], state)
            for p in range(start, start + per_batch):
                first = firsts[p]
                alpha = scal_ref[p, 1:2, 0:1]
                z = scal_ref[p, 2:3, 0:1]
                factor = 1.5 * eye - 0.5 * first[:, 0:nobs]
                second = dot6(factor, state_ref[p])
                state_ref[p, :, 0:2 * nobs] = second[:, 0:2 * nobs]
                q = state_ref[p, :, 2 * nobs:3 * nobs]
                state_ref[p, :, 2 * nobs:3 * nobs] = second[:, 2 * nobs:3 * nobs] - 0.5 * z * (
                    first[:, nobs:2 * nobs] + alpha * (first[:, 2 * nobs:3 * nobs] + z * q))
                scal_ref[p, 2:3, :] = jnp.broadcast_to(z * (1.5 - 0.5 * alpha * z * z), (1, GY))

        for c in range(b * sets // batches, (b + 1) * sets // batches):
            @pl.loop(c * per_set, (c + 1) * per_set)
            def _(p):
                s = scal_ref[p, 0:1, 0:1]
                z = scal_ref[p, 2:3, 0:1]
                scale = lax.rsqrt(s)
                root = state_ref[p, :, nobs:2 * nobs] * scale
                u = u_ref[p]
                once = jnp.sum(root * column(v_ref[p]), axis=0, keepdims=True)
                twice = jnp.sum(root * once, axis=1, keepdims=True)
                w = jnp.sum(u * twice, axis=0, keepdims=True)
                e = xt_ref[p]
                qu = dot3(state_ref[p, :, 2 * nobs:3 * nobs], u) * (math.sqrt(a) * scale / s)
                weights = dot3(u.T, qu)
                shift = mean_ref[p] + jnp.sum(e * w, axis=1, keepdims=True)
                xt_ref[p] = shift + (math.sqrt(a) * scale * z) * e + dot3(e, weights)

            def collect(f):
                t = jnp.concatenate([
                    xt_ref[p, tile_rows(q * chunk + f, cells), h * half:(h + 1) * half]
                    for q in range(sets) for h in range(pack)
                    for p in range(c * per_set, (c + 1) * per_set)], 0).T
                for g in range(count):
                    mine = t[g * share:(g + 1) * share]
                    if size == 1:
                        send_ref[c, :, g, tile_rows(f, size), :] = mine.reshape(sources, 1, GY)
                    else:
                        send_ref[c, :, g, tile_rows(f, size), :] = mine.reshape(sources, size, GY)
            each(chunk, 4, collect)

            if c == 0:
                pl.semaphore_wait(barrier, len(peers))
            for j in range(len(peers)):
                part(c, j).start()
            own(c).start()

    for c in range(sets):
        for j in range(len(peers)):
            part(c, j).wait()
        own(c).wait()


def remote_params(collective_id):
    return pltpu.CompilerParams(vmem_limit_bytes=56 * 2**20, collective_id=collective_id,
                                has_side_effects=True)


def call(kernel, outs, args, scratch=(), params=PARAMS):
    return pl.pallas_call(
        kernel,
        out_shape=[jax.ShapeDtypeStruct(s, F32) for s in outs],
        in_specs=[VMEM] * len(args),
        out_specs=[VMEM] * len(outs),
        scratch_shapes=list(scratch),
        compiler_params=params,
    )(*args)


def shards(ensemble, blending_matrix, lateral_spreading, obs_op, obs_value, obs_precision):
    mem, levels, cols = ensemble.shape
    members = lax.axis_size("member")
    patches, nobs, entries = obs_op.shape
    ens = mem * members
    rows = cols // GY
    pack = GY * members // cols
    count, size = groups_of(mem // pack)
    padded = -(-levels // 16) * 16
    blend = jnp.tile(jnp.pad(blending_matrix, ((0, padded - levels),) * 2), (1, 3))
    rate = lateral_spreading[:, None]
    packed = (members, count, levels * size, GY)
    dma = pltpu.SemaphoreType.DMA
    got, = call(
        forecast_kernel, [packed], (ensemble.transpose(1, 0, 2), blend, rate),
        [
            pltpu.VMEM((2, rows, count, pack, levels * size, GY), F32),
            pltpu.VMEM((NSTEP, count, pack, levels * size, GY), F32),
            pltpu.VMEM((NSTEP, count, pack, levels * size, GY), F32),
            pltpu.VMEM(packed, F32),
            pltpu.VMEM((levels * 8, GY), F32),
            dma((2, NSTEP, count)),
            dma((2, NSTEP, count)),
            dma((count, members)),
            dma((count, members)),
            dma((count,)),
        ],
        remote_params(0))
    sets = min(4, patches)
    parts = (sets, members, count, levels // sets * size, GY)
    back, = call(
        functools.partial(analysis_kernel, levels), [parts],
        (got, obs_op.transpose(0, 2, 1), obs_value, obs_precision),
        [
            pltpu.VMEM((patches, entries, ens), F32),
            pltpu.VMEM((patches, entries, 1), F32),
            pltpu.VMEM((patches, nobs, ens), F32),
            pltpu.VMEM((patches, 1, nobs), F32),
            pltpu.VMEM((patches, nobs, 3 * nobs), F32),
            pltpu.VMEM((patches, 8, GY), F32),
            pltpu.VMEM(parts, F32),
            dma((sets, members - 1)),
            dma((sets, members - 1)),
            dma((sets,)),
        ],
        remote_params(1))
    chunk = levels // sets
    steps = chunk if size % 8 == 0 else 1
    out = pl.pallas_call(
        functools.partial(unpack_kernel, chunk // steps),
        out_shape=jax.ShapeDtypeStruct((sets, chunk, mem, cols), F32),
        grid=(steps,),
        in_specs=[pl.BlockSpec((sets, members, count, chunk // steps * size, GY),
                               lambda i: (0, 0, 0, i, 0))],
        out_specs=pl.BlockSpec((sets, chunk // steps, mem, cols), lambda i: (0, i, 0, 0)),
        compiler_params=PARAMS,
    )(back)
    return out.reshape(levels, mem, cols).transpose(1, 0, 2)


def solution(mesh):
    return jax.shard_map(
        shards,
        mesh=mesh,
        in_specs=(
            P("member", None, "region"),
            P(),
            P(),
            P(("region", "member"), None, None),
            P(("region", "member"), None),
            P(("region", "member"), None),
        ),
        out_specs=P("member", None, "region"),
        check_vma=False,
    )
```

time: 407 us -> 354 us (0.87)
  blocking collectives: 62.3 us -> 0 us
  Pallas kernels: 323 us -> 349 us
  local copies, waits for them, and re-layouts: 21.2 us -> 2.98 us
    all_to_all x1 -> x0, blocking collectives: 62.3 us -> none  [shards(): lax.all_to_all(back, 'member', split_axis=0, concat_axis=0, tiled=True)]
    pallas_call x0 -> x1, Pallas kernels: none -> 15 us  [shards(): pl.pallas_call(functools.partial(unpack_kernel, chunk // steps), out_shap...]
    pallas_call x3 -> x2, Pallas kernels: 323 us -> 334 us  [call(): pl.pallas_call(kernel, out_shape=[jax.ShapeDtypeStruct(s, F32) for s in o...]
    unnamed x13 -> x1, local copies, waits for them, and re-layouts: 9.95 us -> 0.87 us
    pallas_call x1 -> x0, local copies, waits for them, and re-layouts: 7.64 us -> none  [call(): pl.pallas_call(kernel, out_shape=[jax.ShapeDtypeStruct(s, F32) for s in o...]
where the time goes in v3:
time: 354 us; the launch traced here: 352 us
  Pallas kernels  349 us (99%)
    pallas_call x2, Pallas kernels, call(): pl.pallas_call(kernel, out_shape=[jax.ShapeDtypeStruct(s, F32) for s in o...  334 us
    pallas_call x1, Pallas kernels, shards(): pl.pallas_call(functools.partial(unpack_kernel, chunk // steps), out_shap...  15 us

profile of v3, /device:TPU:0, one launch (start us, length us, event | category | flops | bytes accessed | tf_op | source)
XLA Modules:
  0.0 352.1 jit_solution(5350719514186468957)
XLA Ops:
  0.0 0.9 copy.11
  0.9 1.4 copy.10.rate_ref
  2.3 0.7 copy.9.blend_ref
  3.0 248.3 %shard_map.64.x_ref = f32[8,2,608,128]{3,2,1,0:T(8,128)} custom-call(f32[76,32,512]{2,1,0:T(8,128)} %bitcast.7, f32[80,240]{1,0:T(8,128)} %copy.9.blend_ref, f32[76,1]{1,0:T(8,128)} %copy.10.rate_ref), custom_call_target="tpu_custom_call" | custom-call | tf_op jit(solution)/shard_map/pallas_call | solution.py:420
  251.3 85.8 %shard_map.65.x_ref = f32[4,8,2,152,128]{4,3,2,1,0:T(8,128)} custom-call(f32[8,2,608,128]{3,2,1,0:T(8,128)} %shard_map.64.x_ref, f32[8,608,128]{2,1,0:T(8,128)} %bitcast.8, f32[8,128]{1,0:T(8,128)} %val_ref.1, f32[8,128]{1,0:T(8,128)} %prec_ref.1), custom_call_target="tpu_custom_call" | custom-call | tf_op jit(solution)/shard_map/pallas_call | solution.py:420
  337.1 15.0 %shard_map.66 = f32[4,19,32,512]{3,2,1,0:T(8,128)} custom-call(f32[4,8,2,152,128]{4,3,2,1,0:T(8,128)} %shard_map.65.x_ref), custom_call_target="tpu_custom_call" | custom-call | tf_op jit(solution)/shard_map/pallas_call | solution.py:478
  (2 shorter events, 0.0 us)

commit v4 on v3

--- a/solution.py
+++ b/solution.py
@@ -251,24 +251,20 @@
         own(g).wait()
 
 
-def unpack_kernel(chunk, x_ref, o_ref):
-    sets, _, count, packed, _ = x_ref.shape
-    mem, cols = o_ref.shape[2:]
-    rows = cols // GY
-    pack = x_ref.shape[1] // rows
+def unpack_kernel(x_ref, o_ref):
+    sets, pack, count, _, _ = x_ref.shape
+    _, chunk, mem, _ = o_ref.shape
     size = mem // (pack * count)
 
     def body(f):
         for g in range(count):
-            for r in range(rows):
-                tiles = swap_blocks([x_ref[c, r * pack + k, g, tile_rows(f, size), :]
-                                     for k in range(pack) for c in range(sets)])
-                for part in range(sets):
-                    for h in range(pack):
-                        first = (h * count + g) * size
-                        o_ref[part, f, first:first + size, r * GY:(r + 1) * GY] = (
-                            tiles[part * pack + h])
-    each(chunk, 1, body)
+            tiles = swap_blocks([x_ref[c, k, g, tile_rows(f, size), :]
+                                 for k in range(pack) for c in range(sets)])
+            for part in range(sets):
+                for h in range(pack):
+                    first = (h * count + g) * size
+                    o_ref[part, f, first:first + size, :] = tiles[part * pack + h]
+    each(chunk, 4, body)
 
 
 def analysis_kernel(levels, x_ref, op_ref, val_ref, prec_ref, o_ref,
@@ -280,7 +276,7 @@
     sets = o_ref.shape[0]
     per_set = patches // sets
     chunk = levels // sets
-    batches = 2
+    batches = sets
     per_batch = patches // batches
     me, peers = others("member")
     cells = entries // levels
@@ -344,29 +340,31 @@
             square = jnp.sum(gram * gram, keepdims=True).reshape(1, 1)
             s = jnp.sqrt(a * a * ens + 2.0 * a * trace + square)
             alpha = a / s
-            state_ref[p, :, 0:nobs] = alpha * eye + gram / s
-            state_ref[p, :, nobs:2 * nobs] = eye
-            state_ref[p, :, 2 * nobs:3 * nobs] = jnp.zeros_like(eye)
+            system = alpha * eye + gram / s
+            factor = 1.5 * eye - 0.5 * system
+            state_ref[p, :, 0:nobs] = dot6(factor, system)
+            state_ref[p, :, nobs:2 * nobs] = factor
+            state_ref[p, :, 2 * nobs:3 * nobs] = -0.5 * eye
             scal_ref[p, 0:1, :] = jnp.broadcast_to(s, (1, GY))
             scal_ref[p, 1:2, :] = jnp.broadcast_to(alpha, (1, GY))
-            scal_ref[p, 2:3, :] = jnp.ones((1, GY), F32)
-
-        @pl.loop(0, ITERS)
+            scal_ref[p, 2:3, :] = jnp.broadcast_to(1.5 - 0.5 * alpha, (1, GY))
+
+        @pl.loop(1, ITERS)
         def _(k):
             firsts = {}
             for p in range(start, start + per_batch):
-                state = state_ref[p]
+                state = state_ref[p, :, 0:2 * nobs]
                 firsts[p] = dot6(state[:, nobs:2 * nobs], state)
             for p in range(start, start + per_batch):
                 first = firsts[p]
                 alpha = scal_ref[p, 1:2, 0:1]
                 z = scal_ref[p, 2:3, 0:1]
                 factor = 1.5 * eye - 0.5 * first[:, 0:nobs]
-                second = dot6(factor, state_ref[p])
-                state_ref[p, :, 0:2 * nobs] = second[:, 0:2 * nobs]
-                q = state_ref[p, :, 2 * nobs:3 * nobs]
-                state_ref[p, :, 2 * nobs:3 * nobs] = second[:, 2 * nobs:3 * nobs] - 0.5 * z * (
-                    first[:, nobs:2 * nobs] + alpha * (first[:, 2 * nobs:3 * nobs] + z * q))
+                inv = state_ref[p, :, nobs:2 * nobs]
+                mixed = factor - (0.5 * alpha * z) * (inv + z * eye)
+                q = dot6(mixed, state_ref[p, :, 2 * nobs:3 * nobs]) - (0.5 * z) * first[:, nobs:2 * nobs]
+                state_ref[p, :, 0:2 * nobs] = dot6(factor, state_ref[p, :, 0:2 * nobs])
+                state_ref[p, :, 2 * nobs:3 * nobs] = q
                 scal_ref[p, 2:3, :] = jnp.broadcast_to(z * (1.5 - 0.5 * alpha * z * z), (1, GY))
 
         for c in range(b * sets // batches, (b + 1) * sets // batches):
@@ -474,14 +472,12 @@
         ],
         remote_params(1))
     chunk = levels // sets
-    steps = chunk if size % 8 == 0 else 1
     out = pl.pallas_call(
-        functools.partial(unpack_kernel, chunk // steps),
+        unpack_kernel,
         out_shape=jax.ShapeDtypeStruct((sets, chunk, mem, cols), F32),
-        grid=(steps,),
-        in_specs=[pl.BlockSpec((sets, members, count, chunk // steps * size, GY),
-                               lambda i: (0, 0, 0, i, 0))],
-        out_specs=pl.BlockSpec((sets, chunk // steps, mem, cols), lambda i: (0, i, 0, 0)),
+        grid=(rows,),
+        in_specs=[pl.BlockSpec((sets, pack, count, chunk * size, GY), lambda r: (0, r, 0, 0, 0))],
+        out_specs=pl.BlockSpec((sets, chunk, mem, GY), lambda r: (0, 0, 0, r)),
         compiler_params=PARAMS,
     )(back)
     return out.reshape(levels, mem, cols).transpose(1, 0, 2)

time: 354 us -> 341 us (0.963)
  Pallas kernels: 349 us -> 336 us
    pallas_call x2, Pallas kernels: 334 us -> 326 us  [call(): pl.pallas_call(kernel, out_shape=[jax.ShapeDtypeStruct(s, F32) for s in o...]
    pallas_call x1, Pallas kernels: 15 us -> 9.41 us  [shards(): pl.pallas_call(unpack_kernel, out_shape=jax.ShapeDtypeStruct((sets, chunk...]
where the time goes in v4:
time: 341 us; the launch traced here: 339 us
  Pallas kernels  336 us (99%)
    pallas_call x2, Pallas kernels, call(): pl.pallas_call(kernel, out_shape=[jax.ShapeDtypeStruct(s, F32) for s in o...  326 us
    pallas_call x1, Pallas kernels, shards(): pl.pallas_call(unpack_kernel, out_shape=jax.ShapeDtypeStruct((sets, chunk...  9.41 us

profile of v4, /device:TPU:0, one launch (start us, length us, event | category | flops | bytes accessed | tf_op | source)
XLA Modules:
  0.0 338.6 jit_solution(9975077935120435810)
XLA Ops:
  0.0 0.9 copy.11
  0.9 1.4 copy.10.rate_ref
  2.3 0.7 copy.9.blend_ref
  3.0 248.3 %shard_map.64.x_ref = f32[8,2,608,128]{3,2,1,0:T(8,128)} custom-call(f32[76,32,512]{2,1,0:T(8,128)} %bitcast.7, f32[80,240]{1,0:T(8,128)} %copy.9.blend_ref, f32[76,1]{1,0:T(8,128)} %copy.10.rate_ref), custom_call_target="tpu_custom_call" | custom-call | tf_op jit(solution)/shard_map/pallas_call | solution.py:418
  251.3 77.9 %shard_map.65.x_ref = f32[4,8,2,152,128]{4,3,2,1,0:T(8,128)} custom-call(f32[8,2,608,128]{3,2,1,0:T(8,128)} %shard_map.64.x_ref, f32[8,608,128]{2,1,0:T(8,128)} %bitcast.8, f32[8,128]{1,0:T(8,128)} %val_ref.1, f32[8,128]{1,0:T(8,128)} %prec_ref.1), custom_call_target="tpu_custom_call" | custom-call | tf_op jit(solution)/shard_map/pallas_call | solution.py:418
  329.2 9.4 %shard_map.66 = f32[4,19,32,512]{3,2,1,0:T(8,128)} custom-call(f32[4,8,2,152,128]{4,3,2,1,0:T(8,128)} %shard_map.65.x_ref), custom_call_target="tpu_custom_call" | custom-call | tf_op jit(solution)/shard_map/pallas_call | solution.py:475
  (2 shorter events, 0.0 us)
